TPU v7x, 128 devices: a whole 4x4x4 slice. The times are simulated.
128 devices in a mesh: leaf: 32 (over x, y, core), sub: 4 (over z).
Axes of the slice: x: 4, y: 4, z: 4, core: 2. Of those that a mesh axis runs over, the one named last changes fastest.
Arguments:
- density: float32 [8192, 16, 128], P(('leaf', 'sub')), may hold values from -6 to 6
- leaf_basis: bfloat16 [8192, 32, 128], P(('leaf', 'sub')), may hold values from -0.5 to 0.5
- near_tiles: bfloat16 [16384, 128, 128], P(('leaf', 'sub')), may hold values from -0.5 to 0.5
- near_rows: int32 [16384], P(('leaf', 'sub')), may hold values from 0 to 8191, as said below
- near_cols: int32 [16384], P(('leaf', 'sub')), may hold values from 0 to 8191, as said below
- near_count: int32 [128], P(('leaf', 'sub')), may hold values from 16 to 128, as said below
- far_src: int32 [10880, 27], P(('leaf', 'sub')), may hold values from 0 to 8191, as said below
- coupling: bfloat16 [27, 10880, 1024], P(None, ('leaf', 'sub')), may hold values from -0.21875 to 0.21875
- transfer: float32 [10880, 1024], P(('leaf', 'sub')), may hold values from -0.75 to 0.75
- far_src_top: int32 [42, 27], replicated, may hold values from 0 to 31, as said below
- coupling_top: bfloat16 [42, 27, 1024], replicated, may hold values from -0.21875 to 0.21875
- transfer_top: float32 [42, 1024], replicated, may hold values from -0.75 to 0.75
Outputs:
- potential: float32 [8192, 16, 128], P(('leaf', 'sub'))
Inputs may be any that keep to these rules, and one draw needn't show every extreme that they name: `near_rows`: slots of device p name leaves of device p; on every device slot 0 names its first leaf and slot 1 its last leaf. `near_cols`: each entry lies within 32 leaves of the target leaf of its slot; slot 0 names the leaf before its target and slot 1 the leaf after it, where those exist (else the target itself). `near_count`: some device has all 128 slots live. `far_src`: sources of a level-k cluster are level-k clusters at most 64 / 4^k positions away from it; on each device and level, entry 0 of its first cluster is the cluster before it and entry 1 of its last cluster the cluster after it, where those exist (else the cluster itself). `far_src_top`: sources are clusters of the same upper level; on the lowest upper level cluster 0's entry 0 is the level's last cluster and its entry 1 is cluster 0.
All inputs are finite; a program needn't handle non-finite values.
Results may differ from a plain program's by a relative error of at most 0.0003.
Values sent between devices are 32-bit elements; how exact they have to be, the bound alone decides.
No kernel may reach another device: no remote copies, remote signals or barrier semaphores. Data moves between devices by JAX's collectives and lax.ppermute only.
A program may use at most 192 MiB of HBM per device.

v0:
```python
import jax
import jax.numpy as jnp
from jax import lax
from jax.sharding import PartitionSpec as P


def padded_2(cells, sides, width):
    for axis, dim in sides:
        count = lax.axis_size(axis)
        ends = count - 1
        head = lax.slice_in_dim(cells, 0, width, axis=dim)
        tail = lax.slice_in_dim(cells, cells.shape[dim] - width, cells.shape[dim], axis=dim)
        cells = jnp.concatenate(
            [
                lax.ppermute(tail, axis, [(i, (i + 1) % count) for i in range(ends)]),
                cells,
                lax.ppermute(head, axis, [((i + 1) % count, i) for i in range(ends)]),
            ],
            axis=dim,
        )
    return cells


def level_plan(leaf_count, device_count):
    local_sizes = [leaf_count]
    while local_sizes[-1] % 4 == 0:
        local_sizes.append(local_sizes[-1] // 4)
    top_sizes = [device_count * local_sizes[-1] // 4]
    while top_sizes[-1] >= 4:
        top_sizes.append(top_sizes[-1] // 4)
    return (local_sizes, top_sizes)


def parent_sum(moments, transfers):
    contrib = jnp.einsum("nsr,nrq->nsq", moments, transfers, precision=lax.Precision.HIGHEST)
    return contrib.reshape((-1, 4) + contrib.shape[1:]).sum(axis=1)


def child_push(parents, transfers):
    repeated = jnp.repeat(parents, 4, axis=0)
    return jnp.einsum("nsq,nrq->nsr", repeated, transfers, precision=lax.Precision.HIGHEST)


def couple_terms(moments, sources, matrices):
    rank_size = moments.shape[2]
    gathered = jnp.take(moments, sources, axis=0)
    shaped = matrices.astype(jnp.float32).reshape(matrices.shape[:2] + (rank_size, rank_size))
    return jnp.einsum("nfrq,nfsq->nsr", shaped, gathered, precision=lax.Precision.HIGHEST)


def couple_rows(buffer_rows, position, matrices, rhs_count, rank_size):
    total = jnp.zeros((position.shape[0], rhs_count, rank_size), jnp.float32)
    for entry in range(position.shape[1]):
        gathered = jnp.take(buffer_rows, position[:, entry], axis=0).reshape(
            -1, rhs_count, rank_size
        )
        shaped = matrices[entry].astype(jnp.float32).reshape(-1, rank_size, rank_size)
        total = total + jnp.einsum(
            "nsq,nrq->nsr", gathered, shaped, precision=lax.Precision.HIGHEST
        )
    return total


def crown_solve(first_moments, top_sizes, sources, matrices, transfers):
    rank_size = first_moments.shape[2]
    offsets = [sum(top_sizes[:level_idx]) for level_idx in range(len(top_sizes))]

    def trans_of(level_idx):
        begin_at = offsets[level_idx]
        return transfers[begin_at : begin_at + top_sizes[level_idx]].reshape(
            -1, rank_size, rank_size
        )

    moment_list = [first_moments]
    for level_idx in range(len(top_sizes) - 1):
        moment_list.append(parent_sum(moment_list[level_idx], trans_of(level_idx)))
    fields = []
    for level_idx in range(len(top_sizes)):
        begin_at = offsets[level_idx]
        end_at = begin_at + top_sizes[level_idx]
        fields.append(
            couple_terms(
                moment_list[level_idx], sources[begin_at:end_at], matrices[begin_at:end_at]
            )
        )
    coeffs = fields[-1]
    for level_idx in reversed(range(len(top_sizes) - 1)):
        coeffs = fields[level_idx] + child_push(coeffs, trans_of(level_idx))
    return coeffs


def near_field(
    padded,
    rim_width,
    near_tiles,
    near_rows,
    near_cols,
    near_count,
    device,
    leaf_count,
    rhs_count,
    leaf_width,
):
    highest = lax.Precision.HIGHEST
    tile_total = near_tiles.shape[0]
    block_size = tile_total // max(1, leaf_count // 16)
    live_count = near_count[0]
    turn_count = (live_count + block_size - 1) // block_size
    local_rows = near_rows - device * leaf_count
    padded_cols = near_cols - (device * leaf_count - rim_width)
    slot_ids = jnp.arange(block_size, dtype=jnp.int32)
    target_ids = jnp.arange(leaf_count, dtype=jnp.int32)

    def near_block(turn_idx, running):
        first_slot = turn_idx * block_size
        tile_set = lax.dynamic_slice_in_dim(near_tiles, first_slot, block_size, 0)
        row_set = lax.dynamic_slice_in_dim(local_rows, first_slot, block_size, 0)
        col_set = lax.dynamic_slice_in_dim(padded_cols, first_slot, block_size, 0)
        alive_mask = first_slot + slot_ids < live_count
        sources = jnp.take(padded, col_set, axis=0)
        products = jnp.einsum(
            "tsj,tij->tsi", sources, tile_set.astype(jnp.float32), precision=highest
        )
        selector = ((row_set[None, :] == target_ids[:, None]) & alive_mask[None, :]).astype(
            jnp.float32
        )
        return running + jnp.dot(selector, products.reshape(block_size, -1), precision=highest)

    near_part = lax.fori_loop(
        0, turn_count, near_block, jnp.zeros((leaf_count, rhs_count * leaf_width), jnp.float32)
    )
    return near_part.reshape(leaf_count, rhs_count, leaf_width)


def body(
    density,
    leaf_basis,
    near_tiles,
    near_rows,
    near_cols,
    near_count,
    far_src,
    coupling,
    transfer,
    far_src_top,
    coupling_top,
    transfer_top,
):
    highest = lax.Precision.HIGHEST
    leaf_count = density.shape[0]
    rhs_count = density.shape[1]
    leaf_width = density.shape[2]
    rank_size = leaf_basis.shape[1]
    device_count = lax.axis_size("leaf") * lax.axis_size("sub")
    device = lax.axis_index(("leaf", "sub"))
    local_sizes, top_sizes = level_plan(leaf_count, device_count)
    starts = [sum(local_sizes[:level_idx]) for level_idx in range(len(local_sizes))]
    last_level = len(local_sizes) - 1

    def level_part(array, level_idx):
        return array[starts[level_idx] : starts[level_idx] + local_sizes[level_idx]]

    def level_trans(level_idx):
        return level_part(transfer, level_idx).reshape(-1, rank_size, rank_size)

    basis_wide = leaf_basis.astype(jnp.float32)
    moment_list = [jnp.einsum("csj,crj->csr", density, basis_wide, precision=highest)]
    for level_idx in range(last_level):
        moment_list.append(parent_sum(moment_list[level_idx], level_trans(level_idx)))
    crown_terms = jnp.einsum(
        "nsr,nrq->nsq", moment_list[last_level], level_trans(last_level), precision=highest
    )
    flat_terms = crown_terms.reshape(crown_terms.shape[0], rhs_count * rank_size)
    grouped = lax.all_gather(flat_terms, ("leaf", "sub"), axis=0, tiled=True)
    crown_first = grouped.reshape(-1, 4, rhs_count * rank_size).sum(axis=1)
    crown_first = crown_first.reshape(-1, rhs_count, rank_size)
    crown_coeffs = crown_solve(crown_first, top_sizes, far_src_top, coupling_top, transfer_top)
    level_fields = []
    rim_width = leaf_count // 2
    padded = padded_2(density, ((("leaf", "sub"), 0),), rim_width)
    near_part = near_field(
        padded,
        rim_width,
        near_tiles,
        near_rows,
        near_cols,
        near_count,
        device,
        leaf_count,
        rhs_count,
        leaf_width,
    )
    for level_idx in range(len(local_sizes)):
        level_size = local_sizes[level_idx]
        rows_here = moment_list[level_idx].reshape(level_size, -1)
        buffer_level = padded_2(rows_here, ((("leaf", "sub"), 0),), level_size)
        position = level_part(far_src, level_idx) - (device - 1) * level_size
        level_fields.append(
            couple_rows(
                buffer_level,
                position,
                coupling[:, starts[level_idx] : starts[level_idx] + local_sizes[level_idx]],
                rhs_count,
                rank_size,
            )
        )
    top_level_size = local_sizes[last_level]
    parent_index = (device * top_level_size + jnp.arange(top_level_size, dtype=jnp.int32)) // 4
    parent_coeffs = jnp.take(crown_coeffs, parent_index, axis=0)
    coeffs = level_fields[last_level] + jnp.einsum(
        "nsq,nrq->nsr", parent_coeffs, level_trans(last_level), precision=highest
    )
    for level_idx in reversed(range(last_level)):
        coeffs = level_fields[level_idx] + child_push(coeffs, level_trans(level_idx))
    far_part = jnp.einsum("csr,cri->csi", coeffs, basis_wide, precision=highest)
    return near_part + far_part


def solution(mesh):
    placed = (
        P(("leaf", "sub"), None, None),
        P(("leaf", "sub"), None, None),
        P(("leaf", "sub"), None, None),
        P(("leaf", "sub")),
        P(("leaf", "sub")),
        P(("leaf", "sub")),
        P(("leaf", "sub"), None),
        P(None, ("leaf", "sub"), None),
        P(("leaf", "sub"), None),
        P(),
        P(),
        P(),
    )
    return jax.shard_map(
        body, mesh=mesh, in_specs=placed, out_specs=P(("leaf", "sub"), None, None), check_vma=False
    )
```

profile of v0, /device:TPU:121, one launch (start us, length us, event | category | flops | bytes accessed | tf_op | source)
XLA Modules:
  0.0 762.4 jit_solution(9988310144618004038)
XLA Ops:
  1.0 2.0 fusion.90
  4.0 2.0 collective-permute-start.3
  6.1 7.8 %collective-permute-start.2 = (f32[64,512]{1,0:T(8,128)}, f32[64,512]{1,0:T(8,128)}, u32[]{:S(2)}, u32[]{:S(2)}) collective-permute-start(f32[64,512]{1,0:T(8,128)} %copy.90), channel_id=1, source_target_pairs={{0,1},{1,2},{2,3},{3,4},{4,5},{5,6},{6,7},{7,8},{8,9},{9,10},{10,1... | collective-permute-start | bytes 393224 | tf_op jit(solution)/shard_map/ppermute | solution.py:15
  18.5 1.9 collective-permute-start.9
  20.4 7.9 %collective-permute-start.8 = (f32[1,512]{1,0:T(1,128)}, f32[1,512]{1,0:T(1,128)}, u32[]{:S(2)}, u32[]{:S(2)}) collective-permute-start(f32[1,512]{1,0:T(1,128)} %reshape.1266), channel_id=1, source_target_pairs={{0,1},{1,2},{2,3},{3,4},{4,5},{5,6},{6,7},{7,8},{8,9},{9,10},{10,1... | collective-permute-start | bytes 6152 | tf_op jit(solution)/shard_map/ppermute | solution.py:15
  28.4 2.1 collective-permute-start.7
  31.9 3.0 fusion.85
  34.9 2.3 fusion.86
  39.4 1.6 fusion.84
  41.0 1.9 fusion.83
  45.9 1.6 fusion.81
  55.3 1.8 slice_reduce_fusion.1
  107.5 1.7 slice.1053
  109.9 2.9 slice.1047
  149.5 2.0 copy.140
  151.7 1.6 copy.144
  154.3 1.6 copy.148
  185.7 1.6 reshape.1157
  188.5 1.6 reshape.1155
  191.1 1.6 reshape.1161
  194.2 1.6 reshape.1165
  195.8 1.6 reshape.1167
  197.4 1.6 reshape.1169
  199.0 1.6 reshape.1171
  201.4 1.6 reshape.1175
  203.0 1.6 reshape.1177
  204.6 1.6 reshape.1179
  206.1 1.6 reshape.1181
  207.7 1.6 reshape.1183
  209.3 1.6 reshape.1185
  210.9 1.6 reshape.1187
  214.0 1.6 reshape.1191
  215.6 1.6 reshape.1193
  217.2 1.6 reshape.1195
  218.8 1.6 reshape.1197
  220.4 1.6 reshape.1199
  221.9 1.6 reshape.1201
  223.5 1.6 reshape.1203
  274.9 2.6 reshape.1328
  277.7 62.0 %all-gather = f32[128,1,512]{2,1,0:T(1,128)S(1)} all-gather(f32[1,1,512]{2,1,0:T(1,128)S(1)} %reshape.2393), channel_id=1, replica_groups=mesh['leaf'=32,'sub'=4] {'leaf','sub'}, dimensions={0}, use_global_device_ids=true | all-gather | bytes 264192 | tf_op jit(solution)/shard_map/all_gather | solution.py:174
  343.8 1.9 reshape.1331
  346.5 2.2 gather_fusion.2
  351.1 3.6 fusion.31
  354.7 1.7 convolution_bitcast_fusion
  356.8 1.6 fusion.96
  358.4 9.3 %reshape.1325 = bf16[32,27,32,32]{3,2,0,1:T(8,128)(2,1)} reshape(bf16[32,27,1024]{2,0,1:T(8,128)(2,1)} %slice.1047) | data formatting | bytes 3538944 | tf_op jit(solution)/shard_map/reshape | solution.py:47
  368.3 4.3 gather_fusion.1
  405.5 9.2 %fusion.26 = f32[32,16,32]{2,1,0:T(8,128)S(1)} fusion(bf16[32,27,32,32]{3,2,0,1:T(8,128)(2,1)} %reshape.1325, f32[32,27,16,32]{3,2,1,0:T(8,128)} %bitcast.834, pred[32,27]{1,0:T(8,128)(4,1)S(1)} %copy.203), kind=kOutput, calls=%fused_computation.142 | convolution fusion | flops 170311680 | bytes 3605344 | tf_op jit(solution)/shard_map/nfrq,nfsq->nsr/dot_general | solution.py:48
  415.1 4.0 collective-permute-start.6
  419.1 3.0 collective-permute-start.4
  483.1 2.7 collective-permute-start.5
  485.9 1.9 collective-permute-start.1
  561.8 7.9 %collective-permute-start = (f32[32,16,128]{2,1,0:T(8,128)}, f32[32,16,128]{2,1,0:T(8,128)}, u32[]{:S(2)}, u32[]{:S(2)}) collective-permute-start(f32[32,16,128]{2,1,0:T(8,128)} %get-tuple-element.421), channel_id=1, source_target_pairs={{0,1},{1,2},{2,3},{3,4},{4,5},{5,6},{6,7},{7,8},{8,9},{9,10},{10,1... | collective-permute-start | bytes 786440 | tf_op jit(solution)/shard_map/ppermute | solution.py:15
  704.4 2.1 fusion.91
  706.5 2.2 convolution_add_fusion.28
  708.7 2.2 convolution_add_fusion.27
  710.9 2.2 convolution_add_fusion.26
  713.2 2.2 convolution_add_fusion.25
  736.8 2.5 convolution_add_fusion.1
  740.7 20.0 %while.13 = (s32[]{:T(128)}, f32[64,2048]{1,0:T(8,128)S(1)}, s32[]{:T(128)}, s32[128]{0:T(128)S(1)}, s32[]{:T(128)}, /*index=5*/s32[128]{0:T(128)S(1)}, f32[128,...) while((s32[]{:T(128)}, f32[64,2048]{1,0:T(8,128)S(1)}, ...), condition=%wide.region_1.0_spmd.clone, body=%wide.region_0.0_spmd.clone.sunk | while | flops 151196928 | bytes 3413183 | solution.py:129
  742.1 3.0 fusion.348
  747.1 3.0 fusion.348
  752.1 3.0 fusion.348
  757.1 3.0 fusion.348
  (1132 shorter events, 484.3 us)
Async XLA Ops:
  4.0 643.5 %collective-permute-start.3 = (f32[64,512]{1,0:T(8,128)}, f32[64,512]{1,0:T(8,128)}, u32[]{:S(2)}, u32[]{:S(2)}) collective-permute-start(f32[64,512]{1,0:T(8,128)} %copy.90), channel_id=1, source_target_pairs={{1,0},{2,1},{3,2},{4,3},{5,4},{6,5},{7,6},{8,7},{9,8},{10,9},{11,1... | collective-permute-start | bytes 393224 | tf_op jit(solution)/shard_map/ppermute | solution.py:17
  6.1 641.5 %collective-permute-start.2 = (f32[64,512]{1,0:T(8,128)}, f32[64,512]{1,0:T(8,128)}, u32[]{:S(2)}, u32[]{:S(2)}) collective-permute-start(f32[64,512]{1,0:T(8,128)} %copy.90), channel_id=1, source_target_pairs={{0,1},{1,2},{2,3},{3,4},{4,5},{5,6},{6,7},{7,8},{8,9},{9,10},{10,1... | collective-permute-start | bytes 393224 | tf_op jit(solution)/shard_map/ppermute | solution.py:15
  18.5 396.6 %collective-permute-start.9 = (f32[1,512]{1,0:T(1,128)}, f32[1,512]{1,0:T(1,128)}, u32[]{:S(2)}, u32[]{:S(2)}) collective-permute-start(f32[1,512]{1,0:T(1,128)} %reshape.1266), channel_id=1, source_target_pairs={{1,0},{2,1},{3,2},{4,3},{5,4},{6,5},{7,6},{8,7},{9,8},{10,9},{11,1... | collective-permute-start | bytes 6152 | tf_op jit(solution)/shard_map/ppermute | solution.py:17
  20.4 398.6 %collective-permute-start.8 = (f32[1,512]{1,0:T(1,128)}, f32[1,512]{1,0:T(1,128)}, u32[]{:S(2)}, u32[]{:S(2)}) collective-permute-start(f32[1,512]{1,0:T(1,128)} %reshape.1266), channel_id=1, source_target_pairs={{0,1},{1,2},{2,3},{3,4},{4,5},{5,6},{6,7},{7,8},{8,9},{9,10},{10,1... | collective-permute-start | bytes 6152 | tf_op jit(solution)/shard_map/ppermute | solution.py:15
  28.4 454.8 %collective-permute-start.7 = (f32[4,512]{1,0:T(4,128)S(1)}, f32[4,512]{1,0:T(4,128)}, u32[]{:S(2)}, u32[]{:S(2)}) collective-permute-start(f32[4,512]{1,0:T(4,128)S(1)} %reshape.1210), channel_id=1, source_target_pairs={{1,0},{2,1},{3,2},{4,3},{5,4},{6,5},{7,6},{8,7},{9,8},{10,9},{11,1... | collective-permute-start | bytes 24584 | tf_op jit(solution)/shard_map/ppermute | solution.py:17
  31.9 73.6 %copy-start.48 = (s32[42,27]{0,1:T(8,128)S(1)}, s32[42,27]{0,1:T(8,128)}, u32[]{:S(2)}) copy-start(s32[42,27]{0,1:T(8,128)} %param.31) | copy-start | bytes 13612
  39.4 75.2 %copy-start.52 = (bf16[1,64,1024]{2,1,0:T(8,128)(2,1)S(1)}, bf16[1,64,1024]{2,1,0:T(8,128)(2,1)}, u32[]{:S(2)}) copy-start(bf16[1,64,1024]{2,1,0:T(8,128)(2,1)} %get-tuple-element.395) | copy-start | bytes 393220
  49.1 67.2 %copy-start.219 = (s32[64]{0:T(128)S(1)}, s32[64]{0:T(128)}, u32[]{:S(2)}) copy-start(s32[64]{0:T(128)} %get-tuple-element.595) | copy-start | bytes 772
  49.1 67.8 %copy-start.218 = (s32[64]{0:T(128)S(1)}, s32[64]{0:T(128)}, u32[]{:S(2)}) copy-start(s32[64]{0:T(128)} %get-tuple-element.597) | copy-start | bytes 772
  179.3 95.6 %slice-start = ((bf16[42,27,1024]{2,0,1:T(8,128)(2,1)}), bf16[8,27,1024]{2,0,1:T(8,128)(2,1)S(1)}, s32[]{:S(2)}) async-start(bf16[42,27,1024]{2,0,1:T(8,128)(2,1)} %param.32), calls=%async_computation | async-start | bytes 884736 | tf_op jit(solution)/shard_map/slice | solution.py:83
  182.1 63.5 %copy-start.102 = (bf16[1,4,1024]{2,1,0:T(4,128)(2,1)S(1)}, bf16[1,4,1024]{2,1,0:T(4,128)(2,1)}, u32[]{:S(2)}) copy-start(bf16[1,4,1024]{2,1,0:T(4,128)(2,1)} %get-tuple-element.345) | copy-start | bytes 24580
  182.1 64.2 %copy-start.101 = (bf16[1,4,1024]{2,1,0:T(4,128)(2,1)S(1)}, bf16[1,4,1024]{2,1,0:T(4,128)(2,1)}, u32[]{:S(2)}) copy-start(bf16[1,4,1024]{2,1,0:T(4,128)(2,1)} %get-tuple-element.344) | copy-start | bytes 24580
  182.1 64.9 %copy-start.100 = (bf16[1,4,1024]{2,1,0:T(4,128)(2,1)S(1)}, bf16[1,4,1024]{2,1,0:T(4,128)(2,1)}, u32[]{:S(2)}) copy-start(bf16[1,4,1024]{2,1,0:T(4,128)(2,1)} %get-tuple-element.343) | copy-start | bytes 24580
  182.2 65.6 %copy-start.99 = (bf16[1,4,1024]{2,1,0:T(4,128)(2,1)S(1)}, bf16[1,4,1024]{2,1,0:T(4,128)(2,1)}, u32[]{:S(2)}) copy-start(bf16[1,4,1024]{2,1,0:T(4,128)(2,1)} %get-tuple-element.342) | copy-start | bytes 24580
  184.0 58.8 %copy-start.106 = (bf16[1,4,1024]{2,1,0:T(4,128)(2,1)S(1)}, bf16[1,4,1024]{2,1,0:T(4,128)(2,1)}, u32[]{:S(2)}) copy-start(bf16[1,4,1024]{2,1,0:T(4,128)(2,1)} %get-tuple-element.349) | copy-start | bytes 24580
  184.0 59.5 %copy-start.105 = (bf16[1,4,1024]{2,1,0:T(4,128)(2,1)S(1)}, bf16[1,4,1024]{2,1,0:T(4,128)(2,1)}, u32[]{:S(2)}) copy-start(bf16[1,4,1024]{2,1,0:T(4,128)(2,1)} %get-tuple-element.348) | copy-start | bytes 24580
  184.0 60.2 %copy-start.104 = (bf16[1,4,1024]{2,1,0:T(4,128)(2,1)S(1)}, bf16[1,4,1024]{2,1,0:T(4,128)(2,1)}, u32[]{:S(2)}) copy-start(bf16[1,4,1024]{2,1,0:T(4,128)(2,1)} %get-tuple-element.347) | copy-start | bytes 24580
  184.0 60.9 %copy-start.103 = (bf16[1,4,1024]{2,1,0:T(4,128)(2,1)S(1)}, bf16[1,4,1024]{2,1,0:T(4,128)(2,1)}, u32[]{:S(2)}) copy-start(bf16[1,4,1024]{2,1,0:T(4,128)(2,1)} %get-tuple-element.346) | copy-start | bytes 24580
  185.5 67.7 %copy-start.138 = (bf16[1024]{0:T(1024)(128)(2,1)S(1)}, bf16[1024]{0:T(1024)(128)(2,1)}, u32[]{:S(2)}) copy-start(bf16[1024]{0:T(1024)(128)(2,1)} %get-tuple-element.109) | copy-start | bytes 6148
  185.5 68.4 %copy-start.137 = (bf16[1024]{0:T(1024)(128)(2,1)S(1)}, bf16[1024]{0:T(1024)(128)(2,1)}, u32[]{:S(2)}) copy-start(bf16[1024]{0:T(1024)(128)(2,1)} %get-tuple-element.110) | copy-start | bytes 6148
  185.5 69.1 %copy-start.136 = (bf16[1024]{0:T(1024)(128)(2,1)S(1)}, bf16[1024]{0:T(1024)(128)(2,1)}, u32[]{:S(2)}) copy-start(bf16[1024]{0:T(1024)(128)(2,1)} %get-tuple-element.111) | copy-start | bytes 6148
  185.5 69.8 %copy-start.135 = (bf16[1024]{0:T(1024)(128)(2,1)S(1)}, bf16[1024]{0:T(1024)(128)(2,1)}, u32[]{:S(2)}) copy-start(bf16[1024]{0:T(1024)(128)(2,1)} %get-tuple-element.112) | copy-start | bytes 6148
  185.5 70.4 %copy-start.134 = (bf16[1024]{0:T(1024)(128)(2,1)S(1)}, bf16[1024]{0:T(1024)(128)(2,1)}, u32[]{:S(2)}) copy-start(bf16[1024]{0:T(1024)(128)(2,1)} %get-tuple-element.113) | copy-start | bytes 6148
  185.5 71.1 %copy-start.133 = (bf16[1024]{0:T(1024)(128)(2,1)S(1)}, bf16[1024]{0:T(1024)(128)(2,1)}, u32[]{:S(2)}) copy-start(bf16[1024]{0:T(1024)(128)(2,1)} %get-tuple-element.114) | copy-start | bytes 6148
  185.6 71.8 %copy-start.132 = (bf16[1024]{0:T(1024)(128)(2,1)S(1)}, bf16[1024]{0:T(1024)(128)(2,1)}, u32[]{:S(2)}) copy-start(bf16[1024]{0:T(1024)(128)(2,1)} %get-tuple-element.115) | copy-start | bytes 6148
  185.6 72.4 %copy-start.131 = (bf16[1024]{0:T(1024)(128)(2,1)S(1)}, bf16[1024]{0:T(1024)(128)(2,1)}, u32[]{:S(2)}) copy-start(bf16[1024]{0:T(1024)(128)(2,1)} %get-tuple-element.116) | copy-start | bytes 6148
  185.6 73.1 %copy-start.130 = (bf16[1024]{0:T(1024)(128)(2,1)S(1)}, bf16[1024]{0:T(1024)(128)(2,1)}, u32[]{:S(2)}) copy-start(bf16[1024]{0:T(1024)(128)(2,1)} %get-tuple-element.117) | copy-start | bytes 6148
  185.6 73.8 %copy-start.129 = (bf16[1024]{0:T(1024)(128)(2,1)S(1)}, bf16[1024]{0:T(1024)(128)(2,1)}, u32[]{:S(2)}) copy-start(bf16[1024]{0:T(1024)(128)(2,1)} %get-tuple-element.118) | copy-start | bytes 6148
  185.6 74.4 %copy-start.128 = (bf16[1024]{0:T(1024)(128)(2,1)S(1)}, bf16[1024]{0:T(1024)(128)(2,1)}, u32[]{:S(2)}) copy-start(bf16[1024]{0:T(1024)(128)(2,1)} %get-tuple-element.119) | copy-start | bytes 6148
  185.6 75.1 %copy-start.127 = (bf16[1024]{0:T(1024)(128)(2,1)S(1)}, bf16[1024]{0:T(1024)(128)(2,1)}, u32[]{:S(2)}) copy-start(bf16[1024]{0:T(1024)(128)(2,1)} %get-tuple-element.120) | copy-start | bytes 6148
  185.6 75.8 %copy-start.126 = (bf16[1024]{0:T(1024)(128)(2,1)S(1)}, bf16[1024]{0:T(1024)(128)(2,1)}, u32[]{:S(2)}) copy-start(bf16[1024]{0:T(1024)(128)(2,1)} %get-tuple-element.121) | copy-start | bytes 6148
  185.6 76.4 %copy-start.125 = (bf16[1024]{0:T(1024)(128)(2,1)S(1)}, bf16[1024]{0:T(1024)(128)(2,1)}, u32[]{:S(2)}) copy-start(bf16[1024]{0:T(1024)(128)(2,1)} %get-tuple-element.122) | copy-start | bytes 6148
  185.6 77.1 %copy-start.124 = (bf16[1024]{0:T(1024)(128)(2,1)S(1)}, bf16[1024]{0:T(1024)(128)(2,1)}, u32[]{:S(2)}) copy-start(bf16[1024]{0:T(1024)(128)(2,1)} %get-tuple-element.123) | copy-start | bytes 6148
  185.6 88.5 %copy-start.123 = (bf16[1024]{0:T(1024)(128)(2,1)S(1)}, bf16[1024]{0:T(1024)(128)(2,1)}, u32[]{:S(2)}) copy-start(bf16[1024]{0:T(1024)(128)(2,1)} %get-tuple-element.105) | copy-start | bytes 6148
  185.7 89.1 %copy-start.122 = (f32[1024]{0:T(1024)S(1)}, f32[1024]{0:T(1024)}, u32[]{:S(2)}) copy-start(f32[1024]{0:T(1024)} %slice_reduce_fusion) | copy-start | bytes 12292
  191.1 149.6 %slice-start.1 = ((f32[42,1024]{1,0:T(8,128)}), f32[32,1024]{1,0:T(8,128)S(1)}, s32[]{:S(2)}) async-start(f32[42,1024]{1,0:T(8,128)} %param.33), calls=%async_computation.1 | async-start | bytes 262144 | tf_op jit(solution)/shard_map/slice | solution.py:70
  201.4 144.4 %slice-start.2 = ((f32[42,1024]{1,0:T(8,128)}), f32[8,1024]{1,0:T(8,128)S(1)}, s32[]{:S(2)}) async-start(f32[42,1024]{1,0:T(8,128)} %param.33), calls=%async_computation.2 | async-start | bytes 65536 | tf_op jit(solution)/shard_map/slice | solution.py:70
  414.7 128.5 %copy-start.97 = (bf16[4,32,32]{2,1,0:T(8,128)(2,1)S(1)}, bf16[4,32,32]{2,1,0:T(8,128)(2,1)}, u32[]{:S(2)}) copy-start(bf16[4,32,32]{2,1,0:T(8,128)(2,1)} %reshape.1220) | copy-start | bytes 24580
  414.7 128.7 %copy-start.96 = (bf16[4,32,32]{2,1,0:T(8,128)(2,1)S(1)}, bf16[4,32,32]{2,1,0:T(8,128)(2,1)}, u32[]{:S(2)}) copy-start(bf16[4,32,32]{2,1,0:T(8,128)(2,1)} %reshape.1222) | copy-start | bytes 24580
  414.7 128.8 %copy-start.95 = (bf16[4,32,32]{2,1,0:T(8,128)(2,1)S(1)}, bf16[4,32,32]{2,1,0:T(8,128)(2,1)}, u32[]{:S(2)}) copy-start(bf16[4,32,32]{2,1,0:T(8,128)(2,1)} %reshape.1224) | copy-start | bytes 24580
  414.7 129.0 %copy-start.94 = (bf16[4,32,32]{2,1,0:T(8,128)(2,1)S(1)}, bf16[4,32,32]{2,1,0:T(8,128)(2,1)}, u32[]{:S(2)}) copy-start(bf16[4,32,32]{2,1,0:T(8,128)(2,1)} %reshape.1226) | copy-start | bytes 24580
  414.7 129.9 %copy-start.93 = (bf16[4,32,32]{2,1,0:T(8,128)(2,1)S(1)}, bf16[4,32,32]{2,1,0:T(8,128)(2,1)}, u32[]{:S(2)}) copy-start(bf16[4,32,32]{2,1,0:T(8,128)(2,1)} %reshape.1228) | copy-start | bytes 24580
  414.7 130.8 %copy-start.92 = (bf16[4,32,32]{2,1,0:T(8,128)(2,1)S(1)}, bf16[4,32,32]{2,1,0:T(8,128)(2,1)}, u32[]{:S(2)}) copy-start(bf16[4,32,32]{2,1,0:T(8,128)(2,1)} %reshape.1230) | copy-start | bytes 24580
  414.7 131.8 %copy-start.91 = (bf16[4,32,32]{2,1,0:T(8,128)(2,1)S(1)}, bf16[4,32,32]{2,1,0:T(8,128)(2,1)}, u32[]{:S(2)}) copy-start(bf16[4,32,32]{2,1,0:T(8,128)(2,1)} %reshape.1232) | copy-start | bytes 24580
  414.7 132.7 %copy-start.90 = (bf16[4,32,32]{2,1,0:T(8,128)(2,1)S(1)}, bf16[4,32,32]{2,1,0:T(8,128)(2,1)}, u32[]{:S(2)}) copy-start(bf16[4,32,32]{2,1,0:T(8,128)(2,1)} %reshape.1234) | copy-start | bytes 24580
  414.7 133.6 %copy-start.89 = (bf16[4,32,32]{2,1,0:T(8,128)(2,1)S(1)}, bf16[4,32,32]{2,1,0:T(8,128)(2,1)}, u32[]{:S(2)}) copy-start(bf16[4,32,32]{2,1,0:T(8,128)(2,1)} %reshape.1236) | copy-start | bytes 24580
  414.8 134.5 %copy-start.88 = (bf16[4,32,32]{2,1,0:T(8,128)(2,1)S(1)}, bf16[4,32,32]{2,1,0:T(8,128)(2,1)}, u32[]{:S(2)}) copy-start(bf16[4,32,32]{2,1,0:T(8,128)(2,1)} %reshape.1238) | copy-start | bytes 24580
  414.8 135.4 %copy-start.87 = (bf16[4,32,32]{2,1,0:T(8,128)(2,1)S(1)}, bf16[4,32,32]{2,1,0:T(8,128)(2,1)}, u32[]{:S(2)}) copy-start(bf16[4,32,32]{2,1,0:T(8,128)(2,1)} %reshape.1240) | copy-start | bytes 24580
  414.8 136.4 %copy-start.86 = (bf16[4,32,32]{2,1,0:T(8,128)(2,1)S(1)}, bf16[4,32,32]{2,1,0:T(8,128)(2,1)}, u32[]{:S(2)}) copy-start(bf16[4,32,32]{2,1,0:T(8,128)(2,1)} %reshape.1242) | copy-start | bytes 24580
  414.8 137.3 %copy-start.85 = (bf16[4,32,32]{2,1,0:T(8,128)(2,1)S(1)}, bf16[4,32,32]{2,1,0:T(8,128)(2,1)}, u32[]{:S(2)}) copy-start(bf16[4,32,32]{2,1,0:T(8,128)(2,1)} %reshape.1244) | copy-start | bytes 24580
  414.8 138.2 %copy-start.84 = (bf16[4,32,32]{2,1,0:T(8,128)(2,1)S(1)}, bf16[4,32,32]{2,1,0:T(8,128)(2,1)}, u32[]{:S(2)}) copy-start(bf16[4,32,32]{2,1,0:T(8,128)(2,1)} %reshape.1246) | copy-start | bytes 24580
  414.8 139.1 %copy-start.83 = (bf16[4,32,32]{2,1,0:T(8,128)(2,1)S(1)}, bf16[4,32,32]{2,1,0:T(8,128)(2,1)}, u32[]{:S(2)}) copy-start(bf16[4,32,32]{2,1,0:T(8,128)(2,1)} %reshape.1248) | copy-start | bytes 24580
  414.8 140.1 %copy-start.82 = (bf16[4,32,32]{2,1,0:T(8,128)(2,1)S(1)}, bf16[4,32,32]{2,1,0:T(8,128)(2,1)}, u32[]{:S(2)}) copy-start(bf16[4,32,32]{2,1,0:T(8,128)(2,1)} %reshape.1250) | copy-start | bytes 24580
  414.8 141.0 %copy-start.81 = (bf16[4,32,32]{2,1,0:T(8,128)(2,1)S(1)}, bf16[4,32,32]{2,1,0:T(8,128)(2,1)}, u32[]{:S(2)}) copy-start(bf16[4,32,32]{2,1,0:T(8,128)(2,1)} %reshape.1252) | copy-start | bytes 24580
  414.8 141.9 %copy-start.80 = (bf16[4,32,32]{2,1,0:T(8,128)(2,1)S(1)}, bf16[4,32,32]{2,1,0:T(8,128)(2,1)}, u32[]{:S(2)}) copy-start(bf16[4,32,32]{2,1,0:T(8,128)(2,1)} %reshape.1254) | copy-start | bytes 24580
  414.8 142.8 %copy-start.79 = (bf16[4,32,32]{2,1,0:T(8,128)(2,1)S(1)}, bf16[4,32,32]{2,1,0:T(8,128)(2,1)}, u32[]{:S(2)}) copy-start(bf16[4,32,32]{2,1,0:T(8,128)(2,1)} %reshape.1256) | copy-start | bytes 24580
  414.9 143.8 %copy-start.78 = (bf16[4,32,32]{2,1,0:T(8,128)(2,1)S(1)}, bf16[4,32,32]{2,1,0:T(8,128)(2,1)}, u32[]{:S(2)}) copy-start(bf16[4,32,32]{2,1,0:T(8,128)(2,1)} %reshape.1258) | copy-start | bytes 24580
  414.9 144.7 %copy-start.77 = (bf16[4,32,32]{2,1,0:T(8,128)(2,1)S(1)}, bf16[4,32,32]{2,1,0:T(8,128)(2,1)}, u32[]{:S(2)}) copy-start(bf16[4,32,32]{2,1,0:T(8,128)(2,1)} %reshape.1260) | copy-start | bytes 24580
  414.9 145.6 %copy-start.76 = (bf16[4,32,32]{2,1,0:T(8,128)(2,1)S(1)}, bf16[4,32,32]{2,1,0:T(8,128)(2,1)}, u32[]{:S(2)}) copy-start(bf16[4,32,32]{2,1,0:T(8,128)(2,1)} %reshape.1262) | copy-start | bytes 24580
  415.1 70.8 %collective-permute-start.6 = (f32[4,512]{1,0:T(4,128)S(1)}, f32[4,512]{1,0:T(4,128)}, u32[]{:S(2)}, u32[]{:S(2)}) collective-permute-start(f32[4,512]{1,0:T(4,128)S(1)} %reshape.1210), channel_id=1, source_target_pairs={{0,1},{1,2},{2,3},{3,4},{4,5},{5,6},{6,7},{7,8},{8,9},{9,10},{10,1... | collective-permute-start | bytes 24584 | tf_op jit(solution)/shard_map/ppermute | solution.py:15
  419.1 142.7 %collective-permute-start.4 = (f32[16,512]{1,0:T(8,128)S(1)}, f32[16,512]{1,0:T(8,128)}, u32[]{:S(2)}, u32[]{:S(2)}) collective-permute-start(f32[16,512]{1,0:T(8,128)S(1)} %copy-done.75), channel_id=1, source_target_pairs={{0,1},{1,2},{2,3},{3,4},{4,5},{5,6},{6,7},{7,8},{8,9},{9,10},{10,1... | collective-permute-start | bytes 98312 | tf_op jit(solution)/shard_map/ppermute | solution.py:15
  483.1 87.3 %collective-permute-start.5 = (f32[16,512]{1,0:T(8,128)S(1)}, f32[16,512]{1,0:T(8,128)}, u32[]{:S(2)}, u32[]{:S(2)}) collective-permute-start(f32[16,512]{1,0:T(8,128)S(1)} %copy-done.75), channel_id=1, source_target_pairs={{1,0},{2,1},{3,2},{4,3},{5,4},{6,5},{7,6},{8,7},{9,8},{10,9},{11,1... | collective-permute-start | bytes 98312 | tf_op jit(solution)/shard_map/ppermute | solution.py:17
  485.9 253.4 %collective-permute-start.1 = (f32[32,16,128]{2,1,0:T(8,128)}, f32[32,16,128]{2,1,0:T(8,128)}, u32[]{:S(2)}, u32[]{:S(2)}) collective-permute-start(f32[32,16,128]{2,1,0:T(8,128)} %get-tuple-element.422), channel_id=1, source_target_pairs={{1,0},{2,1},{3,2},{4,3},{5,4},{6,5},{7,6},{8,7},{9,8},{10,9},{11,1... | collective-permute-start | bytes 786440 | tf_op jit(solution)/shard_map/ppermute | solution.py:17
  561.8 177.5 %collective-permute-start = (f32[32,16,128]{2,1,0:T(8,128)}, f32[32,16,128]{2,1,0:T(8,128)}, u32[]{:S(2)}, u32[]{:S(2)}) collective-permute-start(f32[32,16,128]{2,1,0:T(8,128)} %get-tuple-element.421), channel_id=1, source_target_pairs={{0,1},{1,2},{2,3},{3,4},{4,5},{5,6},{6,7},{7,8},{8,9},{9,10},{10,1... | collective-permute-start | bytes 786440 | tf_op jit(solution)/shard_map/ppermute | solution.py:15
  (180 other events, 3162.1 us)
where the time goes:
time: 776 us; the launch traced here: 762 us
  local copies, waits for them, and re-layouts  372 us (48%)
  matrix products  141 us (18%)
  other arithmetic  90.6 us (12%)
  blocking collectives  62 us (8%)
  between operations  55.9 us (7%)
  starting transfers between devices  41.1 us (5%)
    reshape x81, local copies, waits for them, and re-layouts, couple_rows(): matrices[entry].astype(jnp.float32).reshape(-1, rank_size, rank_size)  103 us
    dot_general x108, matrix products, couple_rows(): jnp.einsum('nsq,nrq->nsr', gathered, shaped, precision=lax.Precision.HIGH...  100 us
    reshape x81, local copies, waits for them, and re-layouts, couple_rows(): jnp.take(buffer_rows, position[:, entry], axis=0)  62.2 us
    all_gather x1, blocking collectives, body(): grouped = lax.all_gather(flat_terms, ('leaf', 'sub'), axis=0, tiled=True)  62 us
    another operation x55, local copies, waits for them, and re-layouts  60.2 us
    gather x81, local copies, waits for them, and re-layouts, couple_rows(): jnp.take(buffer_rows, position[:, entry], axis=0)  59.9 us
    gather x46, other arithmetic  40.6 us
    select_n x81, other arithmetic, couple_rows(): jnp.take(buffer_rows, position[:, entry], axis=0)  32.8 us
  transfers between devices with their start and end apart: 10, of which 0 were waited for; matrix products, arithmetic and copies ran while one was open for 76% of the time, Pallas kernels for 0%

commit v1 on v0

v1 whole, which is shorter than its diff:
```python
import jax
import jax.numpy as jnp
from jax import lax
from jax.experimental import pallas as pl
from jax.experimental.pallas import tpu as pltpu
from jax.sharding import PartitionSpec as P

f32, bf16 = jnp.float32, jnp.bfloat16
AXES = ("leaf", "sub")
LEAVES = 64
HALO = 32
NRHS = 16
RANK = 32
FAR = 27
SLOTS = 128
LEVELS = (64, 16, 4, 1)
STARTS = (0, 64, 80, 84)
UPPER = (32, 8, 2)
UPPER_STARTS = (0, 32, 40)
TILES = 22
SPAN = 4 * TILES
PARAMS = pltpu.CompilerParams(vmem_limit_bytes=48 * 1024 * 1024)


def dot_nn(a, b):
    return lax.dot_general(a, b, (((1,), (0,)), ((), ())), preferred_element_type=f32)


def dot_nt(a, b):
    return lax.dot_general(a, b, (((1,), (1,)), ((), ())), preferred_element_type=f32)


def halves(x):
    high = x.astype(bf16)
    return high, (x - high.astype(f32)).astype(bf16)


def stacked(x):
    high, low = halves(x)
    return jnp.concatenate([high, low], axis=0)


def folded(x):
    half = x.shape[0] // 2
    return x[:half] + x[half:]


def grid_of(shape):
    return (
        lax.broadcasted_iota(jnp.int32, shape, 0),
        lax.broadcasted_iota(jnp.int32, shape, 1),
    )


def ones_where(mask):
    return jnp.where(mask, 1.0, 0.0).astype(bf16)


def natural_of(lane):
    return (lane // 32) * 32 + 4 * (lane % 8) + (lane % 32) // 8


def mixing():
    x, y = grid_of((128, 128))
    return ones_where(x == natural_of(y))


def spreading():
    x, y = grid_of((128, 512))
    return ones_where((x // 32 == y // 128) & (x % 32 == y % 32))


def unmixing():
    x, y = grid_of((128, 512))
    return ones_where((x // 32 == y // 128) & (natural_of(x) % 32 == y % 32))


def gathering():
    x, y = grid_of((512, 256))
    lane = y % 128
    entry = jnp.where(y < 128, lane % 32, natural_of(lane) % 32)
    return ones_where((lane // 32 == x // 128) & (entry == x % 32))


def tiling():
    x, y = grid_of((128, 128))
    return ones_where(x % 32 == y % 32)


def lane_groups(rows):
    return lax.broadcasted_iota(jnp.int32, (rows, 128), 1) // 32


def by_group(parts, group):
    out = parts[0]
    for index in range(1, len(parts)):
        out = jnp.where(group == index, parts[index], out)
    return out


def spread_rows(matrix_ref, rows, scratch):
    for first in range(0, rows, 8):
        count = min(8, rows - first)
        block = matrix_ref[first : first + count, :].astype(f32)
        for g in range(8):
            scratch[first // 8, g * 8 : g * 8 + count, :] = block[:, g * 128 : (g + 1) * 128]


def row_of(scratch, row):
    return scratch[row // 8, pl.ds(row % 8, 8, stride=8), :]


def masked_rows(rows8, group8):
    return jnp.concatenate([jnp.where(group8 == r, rows8, 0.0) for r in range(4)], axis=0)


def family(scratch, first, count, group8):
    blocks = [masked_rows(row_of(scratch, first + b), group8) for b in range(count)]
    if count < 4:
        blocks.append(jnp.zeros((32 * (4 - count), 128), f32))
    return halves(jnp.concatenate(blocks, axis=0))


def lifted(high, low, matrices):
    matrix_high, matrix_low = matrices
    return folded(dot_nn(jnp.concatenate([high, low], axis=0), matrix_high)) + dot_nn(
        high, matrix_low
    )


def lowered(coeffs, matrices):
    high, low = halves(coeffs)
    matrix_high, matrix_low = matrices
    return folded(dot_nt(jnp.concatenate([high, low], axis=0), matrix_high)) + dot_nt(
        high, matrix_low
    )


def gathered(parts, gather):
    wide = jnp.concatenate(
        parts + [jnp.zeros((NRHS, 128), f32)] * (4 - len(parts)), axis=1
    )
    both = folded(dot_nn(stacked(wide), gather))
    return both[:, :128], both[:, 128:]


def moments_kernel(density, basis, transfer, right_out, left_out, crown_out, rows):
    group16, group8 = lane_groups(16), lane_groups(8)
    spread_rows(transfer, 85, rows)
    right_out[0:HALO] = density[LEAVES - HALO : LEAVES]
    left_out[0:HALO] = density[0:HALO]
    natural = []
    for i in range(16):
        cells = density[4 * i : 4 * i + 4].reshape(64, 128)
        wide = basis[4 * i : 4 * i + 4].reshape(128, 128)
        found = folded(dot_nt(stacked(cells), wide))
        natural.append(by_group([found[16 * b : 16 * b + 16] for b in range(4)], group16))
    mix = mixing()
    gather = gathering()
    level = jnp.concatenate(natural, axis=0)
    high, low = halves(level)
    high, low = dot_nn(high, mix).astype(bf16), dot_nn(low, mix).astype(bf16)
    tile = 0
    for part in natural:
        right_out[HALO + tile] = part
        left_out[HALO + tile] = part
        tile += 1
    pairs = [(high[16 * i : 16 * i + 16], low[16 * i : 16 * i + 16]) for i in range(16)]
    for size, start in ((64, 0), (16, 64), (4, 80)):
        raised = [
            lifted(pairs[i][0], pairs[i][1], family(rows, start + 4 * i, 4, group8))
            for i in range(size // 4)
        ]
        pairs = []
        for i in range(0, size // 4, 4):
            plain, mixed = gathered(raised[i : i + 4], gather)
            right_out[HALO + tile] = plain
            left_out[HALO + tile] = plain
            tile += 1
            pairs.append(halves(mixed))
    crown = lifted(pairs[0][0], pairs[0][1], family(rows, 84, 1, group8))
    crown = folded(dot_nn(stacked(crown), tiling()))
    packed = by_group([crown[4 * b : 4 * b + 4] for b in range(4)], lane_groups(4))
    for i in range(SLOTS):
        crown_out[i] = packed


def moments_call(density, basis, transfer):
    sent = jax.ShapeDtypeStruct((HALO + TILES, NRHS, 128), f32)
    return pl.pallas_call(
        moments_kernel,
        out_shape=(sent, sent, jax.ShapeDtypeStruct((SLOTS, 4, 128), f32)),
        scratch_shapes=[pltpu.VMEM((11, 64, 128), f32)],
        compiler_params=PARAMS,
        name="moments",
    )(density, basis, transfer)


def local_kernel(
    count,
    near_rows,
    near_cols,
    sources,
    density,
    mine,
    before,
    after,
    tiles,
    coupling,
    near,
    field,
    cells,
    terms,
    rows,
    found,
):
    group8 = lane_groups(8)
    near[...] = jnp.zeros_like(near)

    def from_before(i, carry):
        for u in range(4):
            cells[i * 4 + u] = stacked(before[i * 4 + u])
            cells[HALO + LEAVES + i * 4 + u] = stacked(after[i * 4 + u])
        for u in range(8):
            cells[HALO + i * 8 + u] = stacked(density[i * 8 + u])
        return carry

    lax.fori_loop(0, 8, from_before, 0)
    live = count[0]
    step = 16

    def near_step(turn, carry):
        products = []
        for u in range(step):
            slot = turn * step + u
            product = folded(dot_nt(cells[near_cols[slot]], tiles[slot]))
            products.append(jnp.where(slot < live, product, 0.0))
        for u in range(step):
            row = near_rows[turn * step + u]
            near[row] = near[row] + products[u]
        return carry

    lax.fori_loop(0, (live + step - 1) // step, near_step, 0)

    spread = spreading()
    for place, origin in enumerate((before, mine, after)):

        def spread_terms(i, carry):
            both = stacked(origin[pl.ds(HALO + 2 * i, 2)].reshape(32, 128))
            wide = dot_nn(both, spread).astype(bf16)
            for t in range(2):
                for b in range(4):
                    lanes = slice(b * 128, (b + 1) * 128)
                    at = place * SPAN + (2 * i + t) * 4 + b
                    terms[at, 0:16] = wide[16 * t : 16 * t + 16, lanes]
                    terms[at, 16:32] = wide[32 + 16 * t : 48 + 16 * t, lanes]
            return carry

        lax.fori_loop(0, TILES // 2, spread_terms, 0)

    def couple(first, size):
        base = first if isinstance(first, int) else pl.multiple_of(first, 16)
        for j in range(FAR):
            block = coupling[j, pl.ds(base, size), :].astype(f32)
            for half in range(0, size, 8):
                count8 = min(8, size - half)
                for g in range(8):
                    rows[j, half // 8, g * 8 : g * 8 + count8, :] = block[
                        half : half + count8, g * 128 : (g + 1) * 128
                    ]
        for c in range(size):
            total = jnp.zeros((32, 32), f32)
            for j in range(0, FAR, 2):
                pair = range(j, min(j + 2, FAR))
                left = [
                    masked_rows(
                        rows[jj, c // 8, pl.ds(c % 8, 8, stride=8), :], group8
                    ).astype(bf16)
                    for jj in pair
                ]
                right = [terms[sources[first + c, jj]] for jj in pair]
                total = total + dot_nt(
                    jnp.concatenate(right, axis=1), jnp.concatenate(left, axis=1)
                )
            found[first + c] = folded(total)

    def couple_step(i, carry):
        couple(i * 16, 16)
        return carry

    lax.fori_loop(0, 5, couple_step, 0)
    couple(80, 5)
    for i in range(TILES - 1):
        field[i] = jnp.concatenate([found[4 * i + b] for b in range(4)], axis=1)
    field[TILES - 1] = jnp.concatenate([found[84], jnp.zeros((NRHS, 96), f32)], axis=1)


def local_call(count, near_rows, near_cols, sources, density, mine, before, after, tiles, coupling):
    scalar = pl.BlockSpec(memory_space=pltpu.SMEM)
    vector = pl.BlockSpec(memory_space=pltpu.VMEM)
    return pl.pallas_call(
        local_kernel,
        out_shape=(
            jax.ShapeDtypeStruct((LEAVES, NRHS, 128), f32),
            jax.ShapeDtypeStruct((TILES, NRHS, 128), f32),
        ),
        in_specs=[scalar] * 4 + [vector] * 6,
        out_specs=(vector, vector),
        scratch_shapes=[
            pltpu.VMEM((2 * HALO + LEAVES, 2 * NRHS, 128), bf16),
            pltpu.VMEM((3 * SPAN, 2 * NRHS, 128), bf16),
            pltpu.VMEM((FAR, 2, 64, 128), f32),
            pltpu.VMEM((85, NRHS, RANK), f32),
        ],
        cost_estimate=pl.CostEstimate(
            flops=2_000_000_000, bytes_accessed=40_000_000, transcendentals=0
        ),
        compiler_params=PARAMS,
        name="local",
    )(count, near_rows, near_cols, sources, density, mine, before, after, tiles, coupling)


def crown_kernel(
    place,
    sources,
    terms_in,
    couple0,
    couple1,
    couple2,
    transfer_top,
    transfer,
    basis,
    field,
    near,
    out,
    top_rows,
    own_rows,
    link_rows,
    loose,
    terms,
):
    group8, group16, group32 = lane_groups(8), lane_groups(16), lane_groups(32)
    mix, spread, gather, unmix = mixing(), spreading(), gathering(), unmixing()
    spread_rows(transfer_top, 42, top_rows)
    spread_rows(transfer, 85, own_rows)
    cells = []
    for c in range(32):
        cells.append(
            (terms_in[4 * c] + terms_in[4 * c + 1]) + (terms_in[4 * c + 2] + terms_in[4 * c + 3])
        )
    wide = dot_nn(stacked(jnp.concatenate(cells, axis=0)), spread)
    for c in range(32):
        for b in range(4):
            lanes = slice(b * 128, (b + 1) * 128)
            loose[c, 4 * b : 4 * b + 4] = wide[4 * c : 4 * c + 4, lanes]
            loose[c, 16 + 4 * b : 20 + 4 * b] = wide[128 + 4 * c : 132 + 4 * c, lanes]
    packed = []
    for i in range(8):
        for b in range(4):
            terms[4 * i + b] = loose[4 * i + b].astype(bf16)
        packed.append(by_group([loose[4 * i + b] for b in range(4)], group32).astype(bf16))
    mixed = dot_nn(jnp.concatenate(packed, axis=0), mix).astype(bf16)
    pairs = [(mixed[32 * i : 32 * i + 16], mixed[32 * i + 16 : 32 * i + 32]) for i in range(8)]
    for size, start, at in ((32, 0, 32), (8, 32, 40)):
        raised = [
            lifted(pairs[i][0], pairs[i][1], family(top_rows, start + 4 * i, 4, group8))
            for i in range(size // 4)
        ]
        pairs = []
        for i in range(0, size // 4, 4):
            plain, mixed = gathered(raised[i : i + 4], gather)
            pairs.append(halves(mixed))
            wide = dot_nn(stacked(plain), spread).astype(bf16)
            for b in range(min(4, size // 4)):
                terms[at + i + b] = wide[:, b * 128 : (b + 1) * 128]
    fields = []
    for level, link in enumerate((couple0, couple1, couple2)):
        for first in (0, 16):
            block = link[0, first : min(first + 16, FAR), :].astype(f32)
            for half in (0, 8):
                count = min(8, FAR - first - half)
                for g in range(8):
                    link_rows[level, (first + half) // 8, g * 8 : g * 8 + count, :] = block[
                        half : half + count, g * 128 : (g + 1) * 128
                    ]
        total = jnp.zeros((32, 32), f32)
        for j in range(0, FAR, 2):
            pair = range(j, min(j + 2, FAR))
            left = [
                masked_rows(
                    link_rows[level, jj // 8, pl.ds(jj % 8, 8, stride=8), :], group8
                ).astype(bf16)
                for jj in pair
            ]
            right = [
                terms[UPPER_STARTS[level] + sources[UPPER_STARTS[level] + place[level], jj]]
                for jj in pair
            ]
            total = total + dot_nt(jnp.concatenate(right, axis=1), jnp.concatenate(left, axis=1))
        fields.append(folded(total))

    def one_tiled(mixed):
        padded = jnp.concatenate([mixed, jnp.zeros((NRHS, 96), f32)], axis=1)
        return folded(dot_nn(stacked(padded), unmix[:, 0:128]))

    def top_family(index):
        rows8 = top_rows[index // 8, pl.ds(index % 8, 8, stride=8), :]
        return halves(masked_rows(rows8, group8))

    coeffs = one_tiled(fields[2])
    coeffs = one_tiled(fields[1] + lowered(coeffs, top_family(UPPER_STARTS[1] + place[1])))
    coeffs = one_tiled(fields[0] + lowered(coeffs, top_family(UPPER_STARTS[0] + place[0])))
    parents = [coeffs]
    tile = TILES - 1
    for size, start in ((1, 84), (4, 80), (16, 64), (64, 0)):
        tiles_here = (size + 3) // 4
        first = tile - tiles_here + 1
        children = []
        for i in range(tiles_here):
            matrices = family(own_rows, start + 4 * i, min(4, size), group8)
            mixed = field[first + i] + lowered(parents[i], matrices)
            wide = folded(dot_nn(stacked(mixed), unmix))
            children += [wide[:, b * 128 : (b + 1) * 128] for b in range(min(4, size))]
        parents = children
        tile = first - 1
    for i in range(16):
        blocks = [jnp.where(group16 == b, parents[4 * i + b], 0.0) for b in range(4)]
        far = folded(
            dot_nn(
                stacked(jnp.concatenate(blocks, axis=0)),
                basis[4 * i : 4 * i + 4].reshape(128, 128),
            )
        )
        out[4 * i : 4 * i + 4] = near[4 * i : 4 * i + 4] + far.reshape(4, NRHS, 128)


def crown_call(place, sources, terms, coupling_top, transfer_top, transfer, basis, field, near):
    def whole(array):
        return pl.BlockSpec(array.shape, lambda i, place, sources: (0,) * array.ndim)

    def link(level):
        return pl.BlockSpec(
            (1, FAR, RANK * RANK),
            lambda i, place, sources: (UPPER_STARTS[level] + place[level], 0, 0),
        )

    return pl.pallas_call(
        crown_kernel,
        grid_spec=pltpu.PrefetchScalarGridSpec(
            num_scalar_prefetch=2,
            grid=(1,),
            in_specs=[whole(terms), link(0), link(1), link(2)]
            + [whole(array) for array in (transfer_top, transfer, basis, field, near)],
            out_specs=pl.BlockSpec(
                (LEAVES, NRHS, 128), lambda i, place, sources: (0, 0, 0)
            ),
            scratch_shapes=[
                pltpu.VMEM((6, 64, 128), f32),
                pltpu.VMEM((11, 64, 128), f32),
                pltpu.VMEM((3, 4, 64, 128), f32),
                pltpu.VMEM((32, 32, 128), f32),
                pltpu.VMEM((42, 32, 128), bf16),
            ],
        ),
        out_shape=jax.ShapeDtypeStruct((LEAVES, NRHS, 128), f32),
        compiler_params=PARAMS,
        name="crown",
    )(
        place,
        sources,
        terms,
        coupling_top,
        coupling_top,
        coupling_top,
        transfer_top,
        transfer,
        basis,
        field,
        near,
    )


def body(
    density,
    leaf_basis,
    near_tiles,
    near_rows,
    near_cols,
    near_count,
    far_src,
    coupling,
    transfer,
    far_src_top,
    coupling_top,
    transfer_top,
):
    devices = lax.axis_size("leaf") * lax.axis_size("sub")
    device = lax.axis_index(AXES)
    right, left, crown = moments_call(density, leaf_basis, transfer)
    before = lax.ppermute(right, AXES, [(i, i + 1) for i in range(devices - 1)])
    after = lax.ppermute(left, AXES, [(i + 1, i) for i in range(devices - 1)])
    terms = lax.all_to_all(crown, AXES, 0, 0, tiled=True)

    cluster = jnp.arange(85, dtype=jnp.int32)[:, None]
    shift = jnp.where(cluster < 64, 6, jnp.where(cluster < 80, 4, jnp.where(cluster < 84, 2, 0)))
    start = jnp.where(cluster < 64, 0, jnp.where(cluster < 80, 64, jnp.where(cluster < 84, 80, 84)))
    owner = (far_src >> shift) - (device - 1)
    within = far_src & ((1 << shift) - 1)
    sources = owner * SPAN + start + within

    near, field = local_call(
        near_count,
        near_rows - device * LEAVES,
        near_cols - (device * LEAVES - HALO),
        sources,
        density,
        right,
        before,
        after,
        near_tiles,
        coupling,
    )
    place = jnp.stack([device // 4, device // 16, device // 64]).astype(jnp.int32)
    return crown_call(
        place,
        far_src_top,
        terms,
        coupling_top,
        transfer_top,
        transfer,
        leaf_basis,
        field,
        near,
    )


def solution(mesh):
    placed = (
        P(AXES, None, None),
        P(AXES, None, None),
        P(AXES, None, None),
        P(AXES),
        P(AXES),
        P(AXES),
        P(AXES, None),
        P(None, AXES, None),
        P(AXES, None),
        P(),
        P(),
        P(),
    )
    return jax.shard_map(
        body, mesh=mesh, in_specs=placed, out_specs=P(AXES, None, None), check_vma=False
    )
```

time: 776 us -> 72.2 us (0.09)
  the two profiles are of different devices: /device:TPU:121 before, /device:TPU:6 now
where the time goes in v1:
time: 72.2 us; the launch traced here: 71.6 us
  Pallas kernels  29.1 us (40%)
  starting transfers between devices  20 us (28%)
  local copies, waits for them, and re-layouts  16.1 us (22%)
  waiting for transfers between devices  4.6 us (6%)
  other arithmetic  0.99 us (1%)
  between operations  0.8 us (1%)
    pallas_call x1, Pallas kernels, local_call(): pl.pallas_call(local_kernel, out_shape=(jax.ShapeDtypeStruct((LEAVES, NRH...  18.3 us
    unnamed x31, local copies, waits for them, and re-layouts  16.1 us
    all_to_all x1, starting transfers between devices, body(): terms = lax.all_to_all(crown, AXES, 0, 0, tiled=True)  10.5 us
    pallas_call x1, Pallas kernels, crown_call(): pl.pallas_call(crown_kernel, grid_spec=pltpu.PrefetchScalarGridSpec(num_s...  8.09 us
    ppermute x1, starting transfers between devices, body(): after = lax.ppermute(left, AXES, [(i + 1, i) for i in range(devices - 1)])  7.63 us
    ppermute x1, waiting for transfers between devices, body(): before = lax.ppermute(right, AXES, [(i, i + 1) for i in range(devices - 1)])  4.6 us
    pallas_call x1, Pallas kernels, moments_call(): pl.pallas_call(moments_kernel, out_shape=(sent, sent, jax.ShapeDtypeStruc...  2.74 us
    ppermute x1, starting transfers between devices, body(): before = lax.ppermute(right, AXES, [(i, i + 1) for i in range(devices - 1)])  1.92 us
  transfers between devices with their start and end apart: 3, of which 1 were waited for; matrix products, arithmetic and copies ran while one was open for 10% of the time, Pallas kernels for 26%

profile of v1, /device:TPU:6, one launch (start us, length us, event | category | flops | bytes accessed | tf_op | source)
XLA Modules:
  0.0 71.6 jit_solution(15789651575094708712)
XLA Ops:
  0.0 0.0 copy-start
  0.0 1.0 %copy-done = f32[64,16,128]{2,1,0:T(8,128)S(1)} copy-done((f32[64,16,128]{2,1,0:T(8,128)S(1)}, f32[64,16,128]{2,1,0:T(8,128)}, u32[]{:S(2)}) %copy-start) | copy-done | bytes 524312
  1.0 0.0 copy-start.2
  1.0 1.0 %copy-done.2 = bf16[64,32,128]{2,1,0:T(8,128)(2,1)S(1)} copy-done((bf16[64,32,128]{2,1,0:T(8,128)(2,1)S(1)}, bf16[64,32,128]{2,1,0:T(8,128)(2,1)}, u32[]{:S(2)}) %copy-start.2) | copy-done | bytes 524312
  2.1 0.0 copy-start.4
  2.1 1.0 %copy-done.4 = f32[85,1024]{1,0:T(8,128)S(1)} copy-done((f32[85,1024]{1,0:T(8,128)S(1)}, f32[85,1024]{1,0:T(8,128)}, u32[]{:S(2)}) %copy-start.4) | copy-done | bytes 348184
  3.1 0.0 copy-start.12
  3.1 0.0 copy-start.13
  3.1 0.0 copy-start.1
  3.1 2.7 %moments.1 = (f32[54,16,128]{2,1,0:T(8,128)}, f32[54,16,128]{2,1,0:T(8,128)}, f32[128,4,128]{2,1,0:T(4,128)}) custom-call(f32[64,16,128]{2,1,0:T(8,128)S(1)} %copy-done, bf16[64,32,128]{2,1,0:T(8,128)(2,1)S(1)} %copy-done.2, f32[85,1024]{1,0:T(8,128)S(1)} %copy-done.4), custom_call_target="tpu_custom_call" | custom-call | tf_op jit(solution)/shard_map/moments/pallas_call | solution.py:190
  5.8 10.5 %all-to-all-start = ((f32[128,4,128]{2,1,0:T(4,128)}), f32[128,4,128]{2,1,0:T(4,128)S(1)}, u32[]{:S(2)}, u32[]{:S(2)}) async-start(f32[128,4,128]{2,1,0:T(4,128)} %get-tuple-element.10), calls=%async_computation | async-start | bytes 524288 | tf_op jit(solution)/shard_map/all_to_all | solution.py:502
  16.3 7.6 %collective-permute-start.1 = (f32[54,16,128]{2,1,0:T(8,128)}, f32[54,16,128]{2,1,0:T(8,128)}, u32[]{:S(2)}, u32[]{:S(2)}) collective-permute-start(f32[54,16,128]{2,1,0:T(8,128)} %get-tuple-element.12), channel_id=1, source_target_pairs={{1,0},{2,1},{3,2},{4,3},{5,4},{6,5},{7,6},{8,7},{9,8},{10,9},{11,1... | collective-permute-start | bytes 1327112 | tf_op jit(solution)/shard_map/ppermute | solution.py:501
  23.9 1.9 %collective-permute-start = (f32[54,16,128]{2,1,0:T(8,128)}, f32[54,16,128]{2,1,0:T(8,128)}, u32[]{:S(2)}, u32[]{:S(2)}) collective-permute-start(f32[54,16,128]{2,1,0:T(8,128)} %get-tuple-element.11.mine), channel_id=1, source_target_pairs={{0,1},{1,2},{2,3},{3,4},{4,5},{5,6},{6,7},{7,8},{8,9},{9,10},{10,1... | collective-permute-start | bytes 1327112 | tf_op jit(solution)/shard_map/ppermute | solution.py:500
  26.6 1.4 %copy.22.sources = s32[42,27]{1,0:T(8,128)} copy(s32[42,27]{0,1:T(8,128)} %param.21) | data formatting | bytes 9072 | tf_op args[9]
  28.0 1.4 %copy.19 = s32[85,27]{1,0:T(8,128)} copy(s32[85,27]{0,1:T(8,128)} %param.18) | data formatting | bytes 18360 | tf_op args[6]
  29.4 3.1 %copy.23.couple0.couple1.couple2 = bf16[42,27,1024]{2,1,0:T(8,128)(2,1)S(1)} copy(bf16[42,27,1024]{2,0,1:T(8,128)(2,1)} %param.22) | data formatting | bytes 4644864 | tf_op args[10]
  32.5 0.0 copy-done.12
  32.5 0.0 copy-done.13
  32.5 0.9 %and_add_fusion.sources = s32[85,27]{1,0:T(8,128)S(1)} fusion(s32[85,27]{1,0:T(8,128)} %copy.19, s32[85]{0:T(128)S(1)} %get-tuple-element.16, s32[85]{0:T(128)S(1)} %shift-left_add_fusion, s32[85]{0:T(128)S(1)} %get-tuple-element.15, s32[]{:T(128)S(6)} %sub.45), kind=kLoop, calls=%fused_computation | loop fusion | flops 13770 | bytes 19384 | tf_op jit(solution)/shard_map/add | solution.py:509
  33.4 0.1 pad_add_fusion.place
  33.5 0.0 collective-permute-done.1.after
  33.5 4.6 %collective-permute-done.before = f32[54,16,128]{2,1,0:T(8,128)} collective-permute-done((f32[54,16,128]{2,1,0:T(8,128)}, f32[54,16,128]{2,1,0:T(8,128)}, u32[]{:S(2)}, u32[]{:S(2)}) %collective-permute-start) | collective-permute-done | bytes 442400 | tf_op jit(solution)/shard_map/ppermute | solution.py:500
  38.1 0.0 copy-done.1
  38.1 18.3 %local.1 = (f32[64,16,128]{2,1,0:T(8,128)S(1)}, f32[22,16,128]{2,1,0:T(8,128)S(1)}) custom-call(s32[1]{0:T(128)S(6)} %copy.27.count, s32[128]{0:T(128)S(1)} %get-tuple-element.18.near_rows, s32[128]{0:T(128)S(1)} %get-tuple-element.17.near_cols, s32[85,27]{1,0:T(8,128)S(1)} %and_add_fusion.sources, f32[64,16,128]{2,1,0:T(8,128)S(1)} %copy-done.1, ...), custom_call_target="tpu_custom_call" | custom-call | flops 2000000000 | bytes 40000000 | tf_op jit(solution)/shard_map/local/pallas_call | solution.py:301
  56.4 0.0 copy-start.6
  56.4 0.8 %copy-done.6 = f32[64,16,128]{2,1,0:T(8,128)} copy-done((f32[64,16,128]{2,1,0:T(8,128)}, f32[64,16,128]{2,1,0:T(8,128)S(1)}, u32[]{:S(2)}) %copy-start.6) | copy-done | bytes 524312
  57.2 0.0 copy-start.9
  57.2 0.7 copy-done.9
  57.9 0.0 all-to-all-done.terms_in
  57.9 0.0 copy-start.3
  57.9 1.0 %copy-done.3 = bf16[64,32,128]{2,1,0:T(8,128)(2,1)S(1)} copy-done((bf16[64,32,128]{2,1,0:T(8,128)(2,1)S(1)}, bf16[64,32,128]{2,1,0:T(8,128)(2,1)}, u32[]{:S(2)}) %copy-start.3) | copy-done | bytes 524312
  58.9 0.0 copy-start.5
  58.9 1.0 %copy-done.5 = f32[85,1024]{1,0:T(8,128)S(1)} copy-done((f32[85,1024]{1,0:T(8,128)S(1)}, f32[85,1024]{1,0:T(8,128)}, u32[]{:S(2)}) %copy-start.5) | copy-done | bytes 348184
  59.9 0.0 copy-start.7
  59.9 1.0 %copy-done.7 = f32[64,16,128]{2,1,0:T(8,128)S(1)} copy-done((f32[64,16,128]{2,1,0:T(8,128)S(1)}, f32[64,16,128]{2,1,0:T(8,128)}, u32[]{:S(2)}) %copy-start.7) | copy-done | bytes 524312
  60.9 0.0 copy-start.8
  61.0 0.9 %copy-done.8 = f32[42,1024]{1,0:T(8,128)S(1)} copy-done((f32[42,1024]{1,0:T(8,128)S(1)}, f32[42,1024]{1,0:T(8,128)}, u32[]{:S(2)}) %copy-start.8) | copy-done | bytes 172056
  61.9 0.0 copy-start.10
  61.9 0.9 %copy-done.10 = f32[22,16,128]{2,1,0:T(8,128)S(1)} copy-done((f32[22,16,128]{2,1,0:T(8,128)S(1)}, f32[22,16,128]{2,1,0:T(8,128)}, u32[]{:S(2)}) %copy-start.10) | copy-done | bytes 180248
  62.8 0.0 copy-start.11
  62.8 0.7 %copy-done.11 = s32[42,27]{1,0:T(8,128)S(1)} copy-done((s32[42,27]{1,0:T(8,128)S(1)}, s32[42,27]{1,0:T(8,128)}, u32[]{:S(2)}) %copy-start.11) | copy-done | bytes 4560
  63.5 8.1 %crown.1 = f32[64,16,128]{2,1,0:T(8,128)} custom-call(s32[3]{0:T(128)S(1)} %pad_add_fusion.place, s32[42,27]{1,0:T(8,128)S(1)} %copy-done.11, f32[128,4,128]{2,1,0:T(4,128)S(1)} %all-to-all-done.terms_in, bf16[42,27,1024]{2,1,0:T(8,128)(2,1)S(1)} %copy.23.couple0.couple1.couple2, bf16[42,27,1024]{2,1,0:T(8,128)(2,1)S(1)} %copy.23.couple0.couple1.couple2, ...), custom_call_target="tpu_custom_call" | custom-call | tf_op jit(solution)/shard_map/crown/pallas_call | solution.py:447
  (3 shorter events, 0.0 us)
Async XLA Ops:
  0.0 1.0 %copy-start = (f32[64,16,128]{2,1,0:T(8,128)S(1)}, f32[64,16,128]{2,1,0:T(8,128)}, u32[]{:S(2)}) copy-start(f32[64,16,128]{2,1,0:T(8,128)} %density.3) | copy-start | bytes 1572868
  1.0 1.0 %copy-start.2 = (bf16[64,32,128]{2,1,0:T(8,128)(2,1)S(1)}, bf16[64,32,128]{2,1,0:T(8,128)(2,1)}, u32[]{:S(2)}) copy-start(bf16[64,32,128]{2,1,0:T(8,128)(2,1)} %basis.3) | copy-start | bytes 1572868
  2.1 1.0 %copy-start.4 = (f32[85,1024]{1,0:T(8,128)S(1)}, f32[85,1024]{1,0:T(8,128)}, u32[]{:S(2)}) copy-start(f32[85,1024]{1,0:T(8,128)} %transfer.3) | copy-start | bytes 1044484
  3.1 29.4 %copy-start.12 = (s32[128]{0:T(128)S(1)}, s32[128]{0:T(128)}, u32[]{:S(2)}) copy-start(s32[128]{0:T(128)} %param.16) | copy-start | bytes 1540
  3.1 29.4 %copy-start.13 = (s32[128]{0:T(128)S(1)}, s32[128]{0:T(128)}, u32[]{:S(2)}) copy-start(s32[128]{0:T(128)} %param.15) | copy-start | bytes 1540
  3.1 35.0 %copy-start.1 = (f32[64,16,128]{2,1,0:T(8,128)S(1)}, f32[64,16,128]{2,1,0:T(8,128)}, u32[]{:S(2)}) copy-start(f32[64,16,128]{2,1,0:T(8,128)} %density.3) | copy-start | bytes 1572868
  5.8 52.1 %all-to-all-start = ((f32[128,4,128]{2,1,0:T(4,128)}), f32[128,4,128]{2,1,0:T(4,128)S(1)}, u32[]{:S(2)}, u32[]{:S(2)}) async-start(f32[128,4,128]{2,1,0:T(4,128)} %get-tuple-element.10), calls=%async_computation | async-start | bytes 524288 | tf_op jit(solution)/shard_map/all_to_all | solution.py:502
  16.3 17.2 %collective-permute-start.1 = (f32[54,16,128]{2,1,0:T(8,128)}, f32[54,16,128]{2,1,0:T(8,128)}, u32[]{:S(2)}, u32[]{:S(2)}) collective-permute-start(f32[54,16,128]{2,1,0:T(8,128)} %get-tuple-element.12), channel_id=1, source_target_pairs={{1,0},{2,1},{3,2},{4,3},{5,4},{6,5},{7,6},{8,7},{9,8},{10,9},{11,1... | collective-permute-start | bytes 1327112 | tf_op jit(solution)/shard_map/ppermute | solution.py:501
  23.9 14.2 %collective-permute-start = (f32[54,16,128]{2,1,0:T(8,128)}, f32[54,16,128]{2,1,0:T(8,128)}, u32[]{:S(2)}, u32[]{:S(2)}) collective-permute-start(f32[54,16,128]{2,1,0:T(8,128)} %get-tuple-element.11.mine), channel_id=1, source_target_pairs={{0,1},{1,2},{2,3},{3,4},{4,5},{5,6},{6,7},{7,8},{8,9},{9,10},{10,1... | collective-permute-start | bytes 1327112 | tf_op jit(solution)/shard_map/ppermute | solution.py:500
  56.4 0.8 %copy-start.6 = (f32[64,16,128]{2,1,0:T(8,128)}, f32[64,16,128]{2,1,0:T(8,128)S(1)}, u32[]{:S(2)}) copy-start(f32[64,16,128]{2,1,0:T(8,128)S(1)} %get-tuple-element.14.near) | copy-start | bytes 1572868
  57.2 0.7 copy-start.9
  57.9 1.0 %copy-start.3 = (bf16[64,32,128]{2,1,0:T(8,128)(2,1)S(1)}, bf16[64,32,128]{2,1,0:T(8,128)(2,1)}, u32[]{:S(2)}) copy-start(bf16[64,32,128]{2,1,0:T(8,128)(2,1)} %basis.3) | copy-start | bytes 1572868
  58.9 1.0 %copy-start.5 = (f32[85,1024]{1,0:T(8,128)S(1)}, f32[85,1024]{1,0:T(8,128)}, u32[]{:S(2)}) copy-start(f32[85,1024]{1,0:T(8,128)} %transfer.3) | copy-start | bytes 1044484
  59.9 1.0 %copy-start.7 = (f32[64,16,128]{2,1,0:T(8,128)S(1)}, f32[64,16,128]{2,1,0:T(8,128)}, u32[]{:S(2)}) copy-start(f32[64,16,128]{2,1,0:T(8,128)} %copy-done.6) | copy-start | bytes 1572868
  60.9 0.9 %copy-start.8 = (f32[42,1024]{1,0:T(8,128)S(1)}, f32[42,1024]{1,0:T(8,128)}, u32[]{:S(2)}) copy-start(f32[42,1024]{1,0:T(8,128)} %transfer_top.1) | copy-start | bytes 516100
  61.9 0.9 %copy-start.10 = (f32[22,16,128]{2,1,0:T(8,128)S(1)}, f32[22,16,128]{2,1,0:T(8,128)}, u32[]{:S(2)}) copy-start(f32[22,16,128]{2,1,0:T(8,128)} %copy-done.9) | copy-start | bytes 540676
  62.8 0.7 %copy-start.11 = (s32[42,27]{1,0:T(8,128)S(1)}, s32[42,27]{1,0:T(8,128)}, u32[]{:S(2)}) copy-start(s32[42,27]{1,0:T(8,128)} %copy.22.sources) | copy-start | bytes 13612

commit v2 on v1

--- a/solution.py
+++ b/solution.py
@@ -19,7 +19,8 @@
 UPPER_STARTS = (0, 32, 40)
 TILES = 22
 SPAN = 4 * TILES
-PARAMS = pltpu.CompilerParams(vmem_limit_bytes=48 * 1024 * 1024)
+LOCAL_FLOPS = 2_000_000_000
+PARAMS = pltpu.CompilerParams(vmem_limit_bytes=60 * 1024 * 1024)
 
 
 def dot_nn(a, b):
@@ -144,27 +145,69 @@
     return both[:, :128], both[:, 128:]
 
 
-def moments_kernel(density, basis, transfer, right_out, left_out, crown_out, rows):
+def own_index():
+    return lax.axis_index("leaf") * lax.axis_size("sub") + lax.axis_index("sub")
+
+
+def start_copies(pairs, semaphores):
+    copies = [
+        pltpu.make_async_copy(source, target, semaphores.at[i])
+        for i, (source, target) in enumerate(pairs)
+    ]
+    for copy in copies:
+        copy.start()
+    return copies
+
+
+def moments_kernel(
+    density_in,
+    basis_in,
+    transfer_in,
+    right_out,
+    left_out,
+    crown_out,
+    density,
+    basis,
+    transfer,
+    rows,
+    summed,
+    crown_terms,
+    semaphores,
+):
+    copies = start_copies(
+        [
+            (density_in, density),
+            (basis_in, basis),
+            (transfer_in, transfer),
+        ],
+        semaphores,
+    )
     group16, group8 = lane_groups(16), lane_groups(8)
-    spread_rows(transfer, 85, rows)
-    right_out[0:HALO] = density[LEAVES - HALO : LEAVES]
-    left_out[0:HALO] = density[0:HALO]
+    mix = mixing()
+    gather = gathering()
+    copies[0].wait()
+    for i, (target, first) in enumerate(((right_out, LEAVES - HALO), (left_out, 0))):
+        copy = pltpu.make_async_copy(
+            density.at[pl.ds(first, HALO)], target.at[pl.ds(0, HALO)], semaphores.at[3 + i]
+        )
+        copy.start()
+        copies.append(copy)
+    copies[1].wait()
     natural = []
     for i in range(16):
         cells = density[4 * i : 4 * i + 4].reshape(64, 128)
         wide = basis[4 * i : 4 * i + 4].reshape(128, 128)
         found = folded(dot_nt(stacked(cells), wide))
         natural.append(by_group([found[16 * b : 16 * b + 16] for b in range(4)], group16))
-    mix = mixing()
-    gather = gathering()
     level = jnp.concatenate(natural, axis=0)
     high, low = halves(level)
     high, low = dot_nn(high, mix).astype(bf16), dot_nn(low, mix).astype(bf16)
     tile = 0
     for part in natural:
-        right_out[HALO + tile] = part
-        left_out[HALO + tile] = part
+        summed[tile] = part
         tile += 1
+    copies[2].wait()
+    spread_rows(transfer, 85, rows)
     pairs = [(high[16 * i : 16 * i + 16], low[16 * i : 16 * i + 16]) for i in range(16)]
     for size, start in ((64, 0), (16, 64), (4, 80)):
         raised = [
@@ -174,15 +217,29 @@
         pairs = []
         for i in range(0, size // 4, 4):
             plain, mixed = gathered(raised[i : i + 4], gather)
-            right_out[HALO + tile] = plain
-            left_out[HALO + tile] = plain
+            summed[tile] = plain
             tile += 1
             pairs.append(halves(mixed))
+    for i, target in enumerate((right_out, left_out)):
+        copy = pltpu.make_async_copy(
+            summed, target.at[pl.ds(HALO, TILES)], semaphores.at[5 + i]
+        )
+        copy.start()
+        copies.append(copy)
     crown = lifted(pairs[0][0], pairs[0][1], family(rows, 84, 1, group8))
     crown = folded(dot_nn(stacked(crown), tiling()))
     packed = by_group([crown[4 * b : 4 * b + 4] for b in range(4)], lane_groups(4))
     for i in range(SLOTS):
-        crown_out[i] = packed
+        crown_terms[i] = packed
+    last = pltpu.make_async_copy(crown_terms, crown_out, semaphores.at[7])
+    last.start()
+    for copy in copies[3:] + [last]:
+        copy.wait()
+
+
+HBM = pl.BlockSpec(memory_space=pltpu.HBM)
+VMEM = pl.BlockSpec(memory_space=pltpu.VMEM)
+SMEM = pl.BlockSpec(memory_space=pltpu.SMEM)
 
 
 def moments_call(density, basis, transfer):
@@ -190,7 +247,17 @@
     return pl.pallas_call(
         moments_kernel,
         out_shape=(sent, sent, jax.ShapeDtypeStruct((SLOTS, 4, 128), f32)),
-        scratch_shapes=[pltpu.VMEM((11, 64, 128), f32)],
+        in_specs=[HBM] * 3,
+        out_specs=(HBM,) * 3,
+        scratch_shapes=[
+            pltpu.VMEM((LEAVES, NRHS, 128), f32),
+            pltpu.VMEM((LEAVES, RANK, 128), bf16),
+            pltpu.VMEM((85, RANK * RANK), f32),
+            pltpu.VMEM((11, 64, 128), f32),
+            pltpu.VMEM((TILES, NRHS, 128), f32),
+            pltpu.VMEM((SLOTS, 4, 128), f32),
+            pltpu.SemaphoreType.DMA((8,)),
+        ],
         compiler_params=PARAMS,
         name="moments",
     )(density, basis, transfer)
@@ -200,24 +267,76 @@
     count,
     near_rows,
     near_cols,
-    sources,
+    far_src,
+    density_in,
+    mine_in,
+    before_in,
+    after_in,
+    tiles_in,
+    coupling_in,
+    near_out,
+    field_out,
+    near,
+    field,
     density,
     mine,
     before,
     after,
     tiles,
     coupling,
-    near,
-    field,
     cells,
     terms,
     rows,
     found,
+    places,
+    sources,
+    semaphores,
+    tile_semaphores,
 ):
+    live = count[0]
+    step = 16
+    turns = (live + step - 1) // step
+    device = own_index()
+    copies = start_copies(
+        [(density_in, density), (before_in, before), (after_in, after), (mine_in, mine)],
+        semaphores,
+    )
+
+    def tile_copy(turn):
+        part = pl.ds(turn * step, step)
+        return pltpu.make_async_copy(tiles_in.at[part], tiles.at[part], tile_semaphores.at[turn])
+
+    for turn in range(SLOTS // step):
+
+        @pl.when(turn < turns)
+        def _():
+            tile_copy(turn).start()
+
+    link_copy = pltpu.make_async_copy(coupling_in, coupling, semaphores.at[4])
+    link_copy.start()
+
+    cluster = lax.broadcasted_iota(jnp.int32, (FAR, 85), 1)
+
+    def per_level(values):
+        return jnp.where(
+            cluster < 64,
+            values[0],
+            jnp.where(cluster < 80, values[1], jnp.where(cluster < 84, values[2], values[3])),
+        )
+
+    named = far_src[...]
+    owner = lax.shift_right_logical(named, per_level((6, 4, 2, 0))) - (device - 1)
+    within = named & per_level((63, 15, 3, 0))
+    places[...] = owner * SPAN + per_level(STARTS) + within
+    place_copy = pltpu.make_async_copy(places, sources, semaphores.at[5])
+    place_copy.start()
+
     group8 = lane_groups(8)
     near[...] = jnp.zeros_like(near)
-
-    def from_before(i, carry):
+    for copy in copies:
+        copy.wait()
+
+    def fill_cells(i, carry):
         for u in range(4):
             cells[i * 4 + u] = stacked(before[i * 4 + u])
             cells[HALO + LEAVES + i * 4 + u] = stacked(after[i * 4 + u])
@@ -225,22 +344,7 @@
             cells[HALO + i * 8 + u] = stacked(density[i * 8 + u])
         return carry
 
-    lax.fori_loop(0, 8, from_before, 0)
-    live = count[0]
-    step = 16
-
-    def near_step(turn, carry):
-        products = []
-        for u in range(step):
-            slot = turn * step + u
-            product = folded(dot_nt(cells[near_cols[slot]], tiles[slot]))
-            products.append(jnp.where(slot < live, product, 0.0))
-        for u in range(step):
-            row = near_rows[turn * step + u]
-            near[row] = near[row] + products[u]
-        return carry
-
-    lax.fori_loop(0, (live + step - 1) // step, near_step, 0)
+    lax.fori_loop(0, 8, fill_cells, 0)
 
     spread = spreading()
     for place, origin in enumerate((before, mine, after)):
@@ -257,6 +361,27 @@
             return carry
 
         lax.fori_loop(0, TILES // 2, spread_terms, 0)
+
+    first_row = device * LEAVES
+    first_col = first_row - HALO
+
+    def near_step(turn, carry):
+        tile_copy(turn).wait()
+        products = []
+        for u in range(step):
+            slot = turn * step + u
+            product = folded(dot_nt(cells[near_cols[slot] - first_col], tiles[slot]))
+            products.append(jnp.where(slot < live, product, 0.0))
+        for u in range(step):
+            row = near_rows[turn * step + u] - first_row
+            near[row] = near[row] + products[u]
+        return carry
+
+    lax.fori_loop(0, turns, near_step, 0)
+    near_copy = pltpu.make_async_copy(near, near_out, semaphores.at[6])
+    near_copy.start()
+    place_copy.wait()
+    link_copy.wait()
 
     def couple(first, size):
         base = first if isinstance(first, int) else pl.multiple_of(first, 16)
@@ -278,7 +403,7 @@
                     ).astype(bf16)
                     for jj in pair
                 ]
-                right = [terms[sources[first + c, jj]] for jj in pair]
+                right = [terms[sources[jj, first + c]] for jj in pair]
                 total = total + dot_nt(
                     jnp.concatenate(right, axis=1), jnp.concatenate(left, axis=1)
                 )
@@ -293,61 +418,95 @@
     for i in range(TILES - 1):
         field[i] = jnp.concatenate([found[4 * i + b] for b in range(4)], axis=1)
     field[TILES - 1] = jnp.concatenate([found[84], jnp.zeros((NRHS, 96), f32)], axis=1)
-
-
-def local_call(count, near_rows, near_cols, sources, density, mine, before, after, tiles, coupling):
-    scalar = pl.BlockSpec(memory_space=pltpu.SMEM)
-    vector = pl.BlockSpec(memory_space=pltpu.VMEM)
+    field_copy = pltpu.make_async_copy(field, field_out, semaphores.at[7])
+    field_copy.start()
+    near_copy.wait()
+    field_copy.wait()
+
+
+def local_call(count, near_rows, near_cols, far_src, density, mine, before, after, tiles, coupling):
+    sent = pltpu.VMEM((HALO + TILES, NRHS, 128), f32)
     return pl.pallas_call(
         local_kernel,
         out_shape=(
             jax.ShapeDtypeStruct((LEAVES, NRHS, 128), f32),
             jax.ShapeDtypeStruct((TILES, NRHS, 128), f32),
         ),
-        in_specs=[scalar] * 4 + [vector] * 6,
-        out_specs=(vector, vector),
+        in_specs=[SMEM] * 3 + [VMEM] + [HBM] * 6,
+        out_specs=(HBM, HBM),
         scratch_shapes=[
+            pltpu.VMEM((LEAVES, NRHS, 128), f32),
+            pltpu.VMEM((TILES, NRHS, 128), f32),
+            pltpu.VMEM((LEAVES, NRHS, 128), f32),
+            sent,
+            sent,
+            sent,
+            pltpu.VMEM((SLOTS, 128, 128), bf16),
+            pltpu.VMEM((FAR, 85, RANK * RANK), bf16),
             pltpu.VMEM((2 * HALO + LEAVES, 2 * NRHS, 128), bf16),
             pltpu.VMEM((3 * SPAN, 2 * NRHS, 128), bf16),
             pltpu.VMEM((FAR, 2, 64, 128), f32),
             pltpu.VMEM((85, NRHS, RANK), f32),
+            pltpu.VMEM((FAR, 85), jnp.int32),
+            pltpu.SMEM((FAR, 85), jnp.int32),
+            pltpu.SemaphoreType.DMA((8,)),
+            pltpu.SemaphoreType.DMA((8,)),
         ],
         cost_estimate=pl.CostEstimate(
-            flops=2_000_000_000, bytes_accessed=40_000_000, transcendentals=0
+            flops=LOCAL_FLOPS, bytes_accessed=40_000_000, transcendentals=0
         ),
         compiler_params=PARAMS,
         name="local",
-    )(count, near_rows, near_cols, sources, density, mine, before, after, tiles, coupling)
+    )(count, near_rows, near_cols, far_src, density, mine, before, after, tiles, coupling)
 
 
 def crown_kernel(
-    place,
     sources,
     terms_in,
-    couple0,
-    couple1,
-    couple2,
+    field_in,
+    near_in,
+    coupling_in,
+    transfer_top_in,
+    transfer_in,
+    basis_in,
+    out_hbm,
+    out,
+    given,
+    field,
+    near,
+    coupling,
     transfer_top,
     transfer,
     basis,
-    field,
-    near,
-    out,
     top_rows,
     own_rows,
     link_rows,
     loose,
     terms,
+    semaphores,
 ):
+    copies = start_copies(
+        [
+            (transfer_top_in, transfer_top),
+            (coupling_in, coupling),
+            (transfer_in, transfer),
+            (basis_in, basis),
+            (terms_in, given),
+            (field_in, field),
+            (near_in, near),
+        ],
+        semaphores,
+    )
+    device = own_index()
+    place = (device // 4, device // 16, device // 64)
     group8, group16, group32 = lane_groups(8), lane_groups(16), lane_groups(32)
     mix, spread, gather, unmix = mixing(), spreading(), gathering(), unmixing()
+    copies[0].wait()
     spread_rows(transfer_top, 42, top_rows)
-    spread_rows(transfer, 85, own_rows)
+    copies[4].wait()
     cells = []
     for c in range(32):
-        cells.append(
-            (terms_in[4 * c] + terms_in[4 * c + 1]) + (terms_in[4 * c + 2] + terms_in[4 * c + 3])
-        )
+        cells.append((given[4 * c] + given[4 * c + 1]) + (given[4 * c + 2] + given[4 * c + 3]))
     wide = dot_nn(stacked(jnp.concatenate(cells, axis=0)), spread)
     for c in range(32):
         for b in range(4):
@@ -373,27 +532,31 @@
             wide = dot_nn(stacked(plain), spread).astype(bf16)
             for b in range(min(4, size // 4)):
                 terms[at + i + b] = wide[:, b * 128 : (b + 1) * 128]
+    copies[1].wait()
+    half = pl.multiple_of((place[0] // 16) * 16, 16)
+    upper8 = (place[0] % 16) < 8
+    for j in range(FAR):
+        block = coupling[j, pl.ds(half, 16), :].astype(f32)
+        block = jnp.where(upper8, block[0:8], block[8:16])
+        last = coupling[j, 32:42, :].astype(f32)
+        for g in range(8):
+            lanes = slice(g * 128, (g + 1) * 128)
+            link_rows[0, j, g * 8 : g * 8 + 8, :] = block[:, lanes]
+            link_rows[1, j, g * 8 : g * 8 + 8, :] = last[0:8, lanes]
+            link_rows[2, j, g * 8 : g * 8 + 2, :] = last[8:10, lanes]
     fields = []
-    for level, link in enumerate((couple0, couple1, couple2)):
-        for first in (0, 16):
-            block = link[0, first : min(first + 16, FAR), :].astype(f32)
-            for half in (0, 8):
-                count = min(8, FAR - first - half)
-                for g in range(8):
-                    link_rows[level, (first + half) // 8, g * 8 : g * 8 + count, :] = block[
-                        half : half + count, g * 128 : (g + 1) * 128
-                    ]
+    for level in range(3):
         total = jnp.zeros((32, 32), f32)
         for j in range(0, FAR, 2):
             pair = range(j, min(j + 2, FAR))
             left = [
                 masked_rows(
-                    link_rows[level, jj // 8, pl.ds(jj % 8, 8, stride=8), :], group8
+                    link_rows[level, jj, pl.ds(place[level] % 8, 8, stride=8), :], group8
                 ).astype(bf16)
                 for jj in pair
             ]
             right = [
-                terms[UPPER_STARTS[level] + sources[UPPER_STARTS[level] + place[level], jj]]
+                terms[UPPER_STARTS[level] + sources[jj, UPPER_STARTS[level] + place[level]]]
                 for jj in pair
             ]
             total = total + dot_nt(jnp.concatenate(right, axis=1), jnp.concatenate(left, axis=1))
@@ -410,6 +573,9 @@
     coeffs = one_tiled(fields[2])
     coeffs = one_tiled(fields[1] + lowered(coeffs, top_family(UPPER_STARTS[1] + place[1])))
     coeffs = one_tiled(fields[0] + lowered(coeffs, top_family(UPPER_STARTS[0] + place[0])))
+    copies[2].wait()
+    spread_rows(transfer, 85, own_rows)
+    copies[5].wait()
     parents = [coeffs]
     tile = TILES - 1
     for size, start in ((1, 84), (4, 80), (16, 64), (64, 0)):
@@ -423,6 +589,9 @@
             children += [wide[:, b * 128 : (b + 1) * 128] for b in range(min(4, size))]
         parents = children
         tile = first - 1
+    copies[3].wait()
+    copies[6].wait()
+    sent = []
     for i in range(16):
         blocks = [jnp.where(group16 == b, parents[4 * i + b], 0.0) for b in range(4)]
         far = folded(
@@ -432,52 +601,41 @@
             )
         )
         out[4 * i : 4 * i + 4] = near[4 * i : 4 * i + 4] + far.reshape(4, NRHS, 128)
-
-
-def crown_call(place, sources, terms, coupling_top, transfer_top, transfer, basis, field, near):
-    def whole(array):
-        return pl.BlockSpec(array.shape, lambda i, place, sources: (0,) * array.ndim)
-
-    def link(level):
-        return pl.BlockSpec(
-            (1, FAR, RANK * RANK),
-            lambda i, place, sources: (UPPER_STARTS[level] + place[level], 0, 0),
-        )
-
+        if i % 4 == 3:
+            part = pl.ds(4 * i - 12, 16)
+            sent.append(
+                pltpu.make_async_copy(out.at[part], out_hbm.at[part], semaphores.at[7 + i // 4])
+            )
+            sent[-1].start()
+    for copy in sent:
+        copy.wait()
+
+
+def crown_call(sources, terms, field, near, coupling_top, transfer_top, transfer, basis):
     return pl.pallas_call(
         crown_kernel,
-        grid_spec=pltpu.PrefetchScalarGridSpec(
-            num_scalar_prefetch=2,
-            grid=(1,),
-            in_specs=[whole(terms), link(0), link(1), link(2)]
-            + [whole(array) for array in (transfer_top, transfer, basis, field, near)],
-            out_specs=pl.BlockSpec(
-                (LEAVES, NRHS, 128), lambda i, place, sources: (0, 0, 0)
-            ),
-            scratch_shapes=[
-                pltpu.VMEM((6, 64, 128), f32),
-                pltpu.VMEM((11, 64, 128), f32),
-                pltpu.VMEM((3, 4, 64, 128), f32),
-                pltpu.VMEM((32, 32, 128), f32),
-                pltpu.VMEM((42, 32, 128), bf16),
-            ],
-        ),
         out_shape=jax.ShapeDtypeStruct((LEAVES, NRHS, 128), f32),
+        in_specs=[SMEM] + [HBM] * 7,
+        out_specs=HBM,
+        scratch_shapes=[
+            pltpu.VMEM((LEAVES, NRHS, 128), f32),
+            pltpu.VMEM((SLOTS, 4, 128), f32),
+            pltpu.VMEM((TILES, NRHS, 128), f32),
+            pltpu.VMEM((LEAVES, NRHS, 128), f32),
+            pltpu.VMEM((FAR, 42, RANK * RANK), bf16),
+            pltpu.VMEM((42, RANK * RANK), f32),
+            pltpu.VMEM((85, RANK * RANK), f32),
+            pltpu.VMEM((LEAVES, RANK, 128), bf16),
+            pltpu.VMEM((6, 64, 128), f32),
+            pltpu.VMEM((11, 64, 128), f32),
+            pltpu.VMEM((3, FAR, 64, 128), f32),
+            pltpu.VMEM((32, 32, 128), f32),
+            pltpu.VMEM((42, 32, 128), bf16),
+            pltpu.SemaphoreType.DMA((11,)),
+        ],
         compiler_params=PARAMS,
         name="crown",
-    )(
-        place,
-        sources,
-        terms,
-        coupling_top,
-        coupling_top,
-        coupling_top,
-        transfer_top,
-        transfer,
-        basis,
-        field,
-        near,
-    )
+    )(sources, terms, field, near, coupling_top, transfer_top, transfer, basis)
 
 
 def body(
@@ -495,24 +653,15 @@
     transfer_top,
 ):
     devices = lax.axis_size("leaf") * lax.axis_size("sub")
-    device = lax.axis_index(AXES)
     right, left, crown = moments_call(density, leaf_basis, transfer)
     before = lax.ppermute(right, AXES, [(i, i + 1) for i in range(devices - 1)])
     after = lax.ppermute(left, AXES, [(i + 1, i) for i in range(devices - 1)])
     terms = lax.all_to_all(crown, AXES, 0, 0, tiled=True)
-
-    cluster = jnp.arange(85, dtype=jnp.int32)[:, None]
-    shift = jnp.where(cluster < 64, 6, jnp.where(cluster < 80, 4, jnp.where(cluster < 84, 2, 0)))
-    start = jnp.where(cluster < 64, 0, jnp.where(cluster < 80, 64, jnp.where(cluster < 84, 80, 84)))
-    owner = (far_src >> shift) - (device - 1)
-    within = far_src & ((1 << shift) - 1)
-    sources = owner * SPAN + start + within
-
     near, field = local_call(
         near_count,
-        near_rows - device * LEAVES,
-        near_cols - (device * LEAVES - HALO),
-        sources,
+        near_rows,
+        near_cols,
+        far_src.T,
         density,
         right,
         before,
@@ -520,17 +669,15 @@
         near_tiles,
         coupling,
     )
-    place = jnp.stack([device // 4, device // 16, device // 64]).astype(jnp.int32)
     return crown_call(
-        place,
-        far_src_top,
+        far_src_top.T,
         terms,
-        coupling_top,
+        field,
+        near,
+        jnp.transpose(coupling_top, (1, 0, 2)),
         transfer_top,
         transfer,
         leaf_basis,
-        field,
-        near,
     )
 
 

time: 72.2 us -> 56.7 us (0.79)
  the two profiles are of different devices: /device:TPU:6 before, /device:TPU:21 now
where the time goes in v2:
time: 56.7 us; the launch traced here: 55.7 us
  Pallas kernels  32 us (56%)
  starting transfers between devices  19.7 us (35%)
  waiting for transfers between devices  1.9 us (3%)
  local copies, waits for them, and re-layouts  1.47 us (3%)
  between operations  0.72 us (1%)
    pallas_call x1, Pallas kernels, local_call(): pl.pallas_call(local_kernel, out_shape=(jax.ShapeDtypeStruct((LEAVES, NRH...  17.5 us
    all_to_all x1, starting transfers between devices, body(): terms = lax.all_to_all(crown, AXES, 0, 0, tiled=True)  11.5 us
    pallas_call x1, Pallas kernels, crown_call(): pl.pallas_call(crown_kernel, out_shape=jax.ShapeDtypeStruct((LEAVES, NRHS...  10.4 us
    ppermute x1, starting transfers between devices, body(): after = lax.ppermute(left, AXES, [(i + 1, i) for i in range(devices - 1)])  6.22 us
    pallas_call x1, Pallas kernels, moments_call(): pl.pallas_call(moments_kernel, out_shape=(sent, sent, jax.ShapeDtypeStruc...  3.99 us
    ppermute x1, starting transfers between devices, body(): before = lax.ppermute(right, AXES, [(i, i + 1) for i in range(devices - 1)])  1.92 us
    ppermute x1, waiting for transfers between devices, body(): before = lax.ppermute(right, AXES, [(i, i + 1) for i in range(devices - 1)])  1.9 us
    unnamed x6, local copies, waits for them, and re-layouts  1.47 us
  transfers between devices with their start and end apart: 3, of which 1 were waited for; matrix products, arithmetic and copies ran while one was open for 0% of the time, Pallas kernels for 32%

profile of v2, /device:TPU:21, one launch (start us, length us, event | category | flops | bytes accessed | tf_op | source)
XLA Modules:
  0.0 55.7 jit_solution(1497184465138496902)
XLA Ops:
  0.0 4.0 %moments.1 = (f32[54,16,128]{2,1,0:T(8,128)}, f32[54,16,128]{2,1,0:T(8,128)}, f32[128,4,128]{2,1,0:T(4,128)}) custom-call(f32[64,16,128]{2,1,0:T(8,128)} %density_in.3, bf16[64,32,128]{2,1,0:T(8,128)(2,1)} %basis_in.3, f32[85,1024]{1,0:T(8,128)} %transfer_in.3), custom_call_target="tpu_custom_call" | custom-call | tf_op jit(solution)/shard_map/moments/pallas_call | solution.py:247
  4.0 6.2 %collective-permute-start.1 = (f32[54,16,128]{2,1,0:T(8,128)}, f32[54,16,128]{2,1,0:T(8,128)S(1)}, u32[]{:S(2)}, u32[]{:S(2)}) collective-permute-start(f32[54,16,128]{2,1,0:T(8,128)} %get-tuple-element.12), channel_id=1, source_target_pairs={{1,0},{2,1},{3,2},{4,3},{5,4},{6,5},{7,6},{8,7},{9,8},{10,9},{11,1... | collective-permute-start | bytes 1327112 | tf_op jit(solution)/shard_map/ppermute | solution.py:658
  10.2 1.9 %collective-permute-start = (f32[54,16,128]{2,1,0:T(8,128)}, f32[54,16,128]{2,1,0:T(8,128)S(1)}, u32[]{:S(2)}, u32[]{:S(2)}) collective-permute-start(f32[54,16,128]{2,1,0:T(8,128)} %get-tuple-element.11.mine_in), channel_id=1, source_target_pairs={{0,1},{1,2},{2,3},{3,4},{4,5},{5,6},{6,7},{7,8},{8,9},{9,10},{10,1... | collective-permute-start | bytes 1327112 | tf_op jit(solution)/shard_map/ppermute | solution.py:657
  12.2 11.5 %all-to-all-start = ((f32[128,4,128]{2,1,0:T(4,128)}), f32[128,4,128]{2,1,0:T(4,128)S(1)}, u32[]{:S(2)}, u32[]{:S(2)}) async-start(f32[128,4,128]{2,1,0:T(4,128)} %get-tuple-element.10), calls=%async_computation | async-start | bytes 524288 | tf_op jit(solution)/shard_map/all_to_all | solution.py:659
  24.3 0.0 collective-permute-done.1.after_in
  24.3 0.0 copy-start.1
  24.3 1.9 %collective-permute-done.before_in = f32[54,16,128]{2,1,0:T(8,128)S(1)} collective-permute-done((f32[54,16,128]{2,1,0:T(8,128)}, f32[54,16,128]{2,1,0:T(8,128)S(1)}, u32[]{:S(2)}, u32[]{:S(2)}) %collective-permute-start) | collective-permute-done | bytes 442400 | tf_op jit(solution)/shard_map/ppermute | solution.py:657
  26.2 0.0 copy-start.2
  26.2 0.0 copy-done.1
  26.2 0.8 %copy-done.2 = f32[54,16,128]{2,1,0:T(8,128)} copy-done((f32[54,16,128]{2,1,0:T(8,128)}, f32[54,16,128]{2,1,0:T(8,128)S(1)}, u32[]{:S(2)}) %copy-start.2) | copy-done | bytes 442392
  27.0 17.5 %local.1 = (f32[64,16,128]{2,1,0:T(8,128)}, f32[22,16,128]{2,1,0:T(8,128)}) custom-call(s32[1]{0:T(128)S(6)} %copy.13.count, s32[128]{0:T(128)} %near_rows.1, s32[128]{0:T(128)} %near_cols.1, s32[27,85]{1,0:T(8,128)} %bitcast.4, f32[64,16,128]{2,1,0:T(8,128)} %density_in.3, f32[54,16,128]{2,1,0:T(8,128)} %get-tuple-element.11.mine_in, ...), custom_call_target="tpu_custom_call" | custom-call | flops 2000000000 | bytes 40000000 | tf_op jit(solution)/shard_map/local/pallas_call | solution.py:429
  44.6 0.0 all-to-all-done.terms_in
  44.6 0.0 copy-start
  44.6 0.7 %copy-done = f32[128,4,128]{2,1,0:T(4,128)} copy-done((f32[128,4,128]{2,1,0:T(4,128)}, f32[128,4,128]{2,1,0:T(4,128)S(1)}, u32[]{:S(2)}) %copy-start) | copy-done | bytes 262168
  45.3 10.4 %crown.1 = f32[64,16,128]{2,1,0:T(8,128)} custom-call(s32[27,42]{1,0:T(8,128)} %bitcast.5, f32[128,4,128]{2,1,0:T(4,128)} %copy-done, f32[22,16,128]{2,1,0:T(8,128)} %get-tuple-element.13.field_in, f32[64,16,128]{2,1,0:T(8,128)} %get-tuple-element.14.near_in, bf16[27,42,1024]{2,1,0:T(8,128)(2,1)} %bitcast.3, f32[42,1024]{1,0:T(8,128)} %transfer_top_in.1, ...), custom_call_target="tpu_custom_call" | custom-call | tf_op jit(solution)/shard_map/crown/pallas_call | solution.py:615
Async XLA Ops:
  4.0 20.3 %collective-permute-start.1 = (f32[54,16,128]{2,1,0:T(8,128)}, f32[54,16,128]{2,1,0:T(8,128)S(1)}, u32[]{:S(2)}, u32[]{:S(2)}) collective-permute-start(f32[54,16,128]{2,1,0:T(8,128)} %get-tuple-element.12), channel_id=1, source_target_pairs={{1,0},{2,1},{3,2},{4,3},{5,4},{6,5},{7,6},{8,7},{9,8},{10,9},{11,1... | collective-permute-start | bytes 1327112 | tf_op jit(solution)/shard_map/ppermute | solution.py:658
  10.2 16.0 %collective-permute-start = (f32[54,16,128]{2,1,0:T(8,128)}, f32[54,16,128]{2,1,0:T(8,128)S(1)}, u32[]{:S(2)}, u32[]{:S(2)}) collective-permute-start(f32[54,16,128]{2,1,0:T(8,128)} %get-tuple-element.11.mine_in), channel_id=1, source_target_pairs={{0,1},{1,2},{2,3},{3,4},{4,5},{5,6},{6,7},{7,8},{8,9},{9,10},{10,1... | collective-permute-start | bytes 1327112 | tf_op jit(solution)/shard_map/ppermute | solution.py:657
  12.2 32.4 %all-to-all-start = ((f32[128,4,128]{2,1,0:T(4,128)}), f32[128,4,128]{2,1,0:T(4,128)S(1)}, u32[]{:S(2)}, u32[]{:S(2)}) async-start(f32[128,4,128]{2,1,0:T(4,128)} %get-tuple-element.10), calls=%async_computation | async-start | bytes 524288 | tf_op jit(solution)/shard_map/all_to_all | solution.py:659
  24.3 1.9 %copy-start.1 = (f32[54,16,128]{2,1,0:T(8,128)}, f32[54,16,128]{2,1,0:T(8,128)S(1)}, u32[]{:S(2)}) copy-start(f32[54,16,128]{2,1,0:T(8,128)S(1)} %collective-permute-done.1.after_in) | copy-start | bytes 1327108
  26.2 0.8 %copy-start.2 = (f32[54,16,128]{2,1,0:T(8,128)}, f32[54,16,128]{2,1,0:T(8,128)S(1)}, u32[]{:S(2)}) copy-start(f32[54,16,128]{2,1,0:T(8,128)S(1)} %collective-permute-done.before_in) | copy-start | bytes 1327108
  44.6 0.7 %copy-start = (f32[128,4,128]{2,1,0:T(4,128)}, f32[128,4,128]{2,1,0:T(4,128)S(1)}, u32[]{:S(2)}) copy-start(f32[128,4,128]{2,1,0:T(4,128)S(1)} %all-to-all-done.terms_in) | copy-start | bytes 786436
